TPU v7x, 128 devices: a whole 4x4x4 slice. The times are simulated.
128 devices in a mesh: angle: 4 (over x), slab: 32 (over y, z, core).
Axes of the slice: x: 4, y: 4, z: 4, core: 2. Of those that a mesh axis runs over, the one named last changes fastest.
Arguments:
- projections: float32 [4, 4, 32, 4, 8192], P('angle', None, 'slab'), may hold values from -6 to 6
- band_start: int32 [4, 32], P('angle'), may hold values from 0 to 96
- row_index: int32 [4, 512, 4096], P('angle', 'slab'), may hold values from 0 to 126
- row_frac: float32 [4, 512, 4096], P('angle', 'slab'), may hold values from 0 to 1
- col_index: int32 [4, 4096], P('angle'), may hold values from 0 to 8190
- col_frac: float32 [4, 4096], P('angle'), may hold values from 0 to 1
- distance_weight: float32 [4, 4096], P('angle'), may hold values from 0.5 to 2
Outputs:
- volume: float32 [512, 4096], P('slab', 'angle')
All inputs are finite; a program needn't handle non-finite values.
Results may differ from a plain program's by a relative error of at most 0.0034.
Values may be sent and summed in bfloat16 or wider, within the bound.
A program may use at most 128 MiB of HBM per device.

v0:
```python
import math

import jax
import jax.numpy as jnp
from jax import lax
from jax.sharding import PartitionSpec as P

HIGHEST = lax.Precision.HIGHEST


def circle_table(count, left, right):
    product = left[:, None] * right[None, :] % count
    angle = 2.0 * math.pi / count * product.astype(jnp.float32)
    return (jnp.cos(angle), jnp.sin(angle))


def dft_tables(cols):
    total = 2 * cols
    bits = total.bit_length() - 1
    first = 2 ** (bits // 2)
    second = total // first
    first_ids = jnp.arange(first, dtype=jnp.int32)
    second_ids = jnp.arange(second, dtype=jnp.int32)
    cos_a, sin_a = circle_table(first, first_ids, first_ids)
    cos_b, sin_b = circle_table(second, second_ids, second_ids)
    twist_c, twist_s = circle_table(total, first_ids, second_ids)
    return (cos_a, sin_a, cos_b, sin_b, twist_c, twist_s)


def forward(values, tables):
    cos_a, sin_a, cos_b, sin_b, twist_c, twist_s = tables
    used = values.shape[1]
    first_re = jnp.einsum("rab,ak->rkb", values, cos_a[:used], precision=HIGHEST)
    first_im = -jnp.einsum("rab,ak->rkb", values, sin_a[:used], precision=HIGHEST)
    turned_re = first_re * twist_c + first_im * twist_s
    turned_im = first_im * twist_c - first_re * twist_s
    out_re = jnp.einsum("rkb,bm->rkm", turned_re, cos_b, precision=HIGHEST) + jnp.einsum(
        "rkb,bm->rkm", turned_im, sin_b, precision=HIGHEST
    )
    out_im = jnp.einsum("rkb,bm->rkm", turned_im, cos_b, precision=HIGHEST) - jnp.einsum(
        "rkb,bm->rkm", turned_re, sin_b, precision=HIGHEST
    )
    return (out_re, out_im)


def inverse_real(spec_re, spec_im, tables, keep):
    cos_a, sin_a, cos_b, sin_b, twist_c, twist_s = tables
    total = cos_a.shape[0] * cos_b.shape[0]
    back_re = jnp.einsum("rkm,mb->rkb", spec_re, cos_b, precision=HIGHEST) - jnp.einsum(
        "rkm,mb->rkb", spec_im, sin_b, precision=HIGHEST
    )
    back_im = jnp.einsum("rkm,mb->rkb", spec_im, cos_b, precision=HIGHEST) + jnp.einsum(
        "rkm,mb->rkb", spec_re, sin_b, precision=HIGHEST
    )
    turned_re = back_re * twist_c - back_im * twist_s
    turned_im = back_im * twist_c + back_re * twist_s
    result = jnp.einsum("ka,rkb->rab", cos_a[:, :keep], turned_re, precision=HIGHEST) - jnp.einsum(
        "ka,rkb->rab", sin_a[:, :keep], turned_im, precision=HIGHEST
    )
    return result / total


def ramp_response(cols, tables):
    total = 2 * cols
    first = tables[0].shape[0]
    second = tables[2].shape[0]
    steps = jnp.arange(total, dtype=jnp.int32)
    dist = jnp.minimum(steps, total - steps)
    safe = jnp.maximum(dist, 1).astype(jnp.float32)
    odd_value = -1.0 / (math.pi**2 * safe * safe)
    kernel = jnp.where(
        dist == 0, jnp.float32(0.25), jnp.where(dist % 2 == 1, odd_value, jnp.float32(0.0))
    )
    spec_re, spec_im = forward(kernel.reshape(1, first, second), tables)
    return spec_re[0]


def filter_rows(rows, tables, response):
    count, cols = rows.shape
    first = tables[0].shape[0]
    second = tables[2].shape[0]
    keep = first // 2
    spec_re, spec_im = forward(rows.reshape(count, keep, second), tables)
    result = inverse_real(spec_re * response, spec_im * response, tables, keep)
    return result.reshape(count, cols).astype(jnp.bfloat16)


def cos_weight(det_rows, cols, det_total):
    scale = 2.0 * cols
    across = jnp.arange(cols, dtype=jnp.float32) - (cols - 1) / 2.0
    down = det_rows.astype(jnp.float32) - (det_total - 1) / 2.0
    return scale / jnp.sqrt(scale * scale + across * across + down[..., None] * down[..., None])


def body(projections, band_start, row_index, row_frac, col_index, col_frac, distance_weight):
    slab_count = lax.axis_size("slab")
    my_slab = lax.axis_index("slab")
    proj, bands, single, band, cols = projections.shape
    det_total = bands * slab_count * band
    rows = projections.reshape(proj, bands, band, cols)
    tables = dft_tables(cols)
    response = ramp_response(cols, tables)
    my_start = lax.dynamic_index_in_dim(band_start, my_slab, 1, keepdims=False)
    inner_rows = jnp.arange(band, dtype=jnp.int32)
    wanted = band_start + jnp.mod(my_slab - band_start, slab_count)
    local_band = wanted // slab_count

    def pick_bands(source, picks):
        return source[picks]

    local_ids = jnp.arange(bands, dtype=jnp.int32)
    det_rows = (local_ids[:, None] * slab_count + my_slab) * band + inner_rows[None, :]
    weighted = rows * cos_weight(det_rows, cols, det_total)[None]

    def filter_image(image):
        return filter_rows(image.reshape(bands * band, cols), tables, response).reshape(
            bands, band, cols
        )

    filtered = lax.map(filter_image, weighted)
    outgoing = jax.vmap(pick_bands)(filtered, local_band)
    carried = lax.all_to_all(outgoing, "slab", split_axis=1, concat_axis=1, tiled=True)

    def add_one(volume, items):
        piece, rows_at, rows_frac, cols_at, cols_frac, weights, start = items
        flat = piece.reshape(-1)

        def fetch(row_shift, col_shift):
            row = rows_at + row_shift
            which = row // band
            source = jnp.mod(start + which, slab_count)
            within = row - which * band
            index = (source * band + within) * cols + cols_at[None, :] + col_shift
            return jnp.take(flat, index).astype(jnp.float32)

        across = cols_frac[None, :]
        lower = (1.0 - across) * fetch(0, 0) + across * fetch(0, 1)
        upper = (1.0 - across) * fetch(1, 0) + across * fetch(1, 1)
        mixed = (1.0 - rows_frac) * lower + rows_frac * upper
        return (volume + weights[None, :] * mixed, None)

    planes, voxels = (row_index.shape[1], row_index.shape[2])
    start_volume = jnp.zeros((planes, voxels), jnp.float32)
    partial_value, unused = lax.scan(
        add_one,
        start_volume,
        (carried, row_index, row_frac, col_index, col_frac, distance_weight, my_start),
    )
    return lax.psum_scatter(partial_value, "angle", scatter_dimension=1, tiled=True)


def solution(mesh):
    in_specs = (
        P("angle", None, "slab", None, None),
        P("angle", None),
        P("angle", "slab", None),
        P("angle", "slab", None),
        P("angle", None),
        P("angle", None),
        P("angle", None),
    )
    out_specs = P("slab", "angle")
    return jax.shard_map(body, mesh=mesh, in_specs=in_specs, out_specs=out_specs, check_vma=False)
```

profile of v0, /device:TPU:1, one launch (start us, length us, event | category | flops | bytes accessed | tf_op | source)
XLA Modules:
  0.0 1703.0 jit_solution(17190011085057657833)
XLA Ops:
  6.5 0.3 fusion.92
  6.8 0.3 fusion.93
  7.1 0.3 fusion.90
  7.4 0.5 convolution_negate_fusion.1
  7.9 0.5 fusion.88
  8.5 0.1 add_multiply_fusion
  8.5 0.1 mul.551
  8.6 0.0 copy-done.5
  8.6 0.4 reshape.125
  9.0 1.1 convolution_negate_fusion
  10.0 1.1 fusion.22
  11.1 1.2 fusion.9
  12.4 1.2 fusion.5
  13.6 0.7 fusion.75
  14.3 0.7 convolution_add_fusion.2
  15.0 1.2 fusion.1
  16.3 1.2 fusion.69
  17.5 1.2 fusion
  18.7 1.4 fusion.66
  20.1 1.2 convolution_subtract_fusion
  21.4 1.2 convolution_add_fusion
  22.6 0.8 fusion.14
  23.4 0.0 copy-start.12
  23.4 0.8 fusion.4
  24.3 0.1 convert_element_type.116
  24.4 0.0 copy-done.12
  24.4 3.6 gather_fusion
  28.0 9.7 all-to-all-start
  37.7 0.0 reduce-scatter.2.cloned.1.call-start
  37.8 0.6 constant_dynamic-slice_fusion
  38.4 0.0 copy-done.6
  38.4 0.0 copy-done.10
  38.4 1.3 fusion.52
  39.7 0.0 copy-start.1
  39.7 0.0 copy-start.3
  39.7 0.0 copy-start.7
  39.7 0.1 fusion.49
  39.8 0.1 copy.21
  39.9 0.1 copy.19
  40.0 0.1 copy.20
  40.1 0.3 copy-done.1
  40.4 0.1 copy-done.3
  40.5 0.0 copy-done.7
  40.5 0.6 broadcast_subtract_fusion
  41.1 0.1 copy.22
  41.2 24.8 %all-to-all-done = bf16[1,32,4,8192]{3,2,0,1:T(4,128)(2,1)S(1)} async-done(((bf16[1,32,4,8192]{3,2,0,1:T(4,128)(2,1)}), bf16[1,32,4,8192]{3,2,0,1:T(4,128)(2,1)S(1)}, u32[]{:S(2)}, u32[]{:S(2)}) %all-to-all-start) | async-done | bytes 2097184 | tf_op jit(solution)/shard_map/all_to_all | solution.py:122
  66.0 1.3 copy-done
  67.4 2.1 copy.18
  69.5 402.1 %gather_fusion.3 = bf16[65536]{0:T(1024)(128)(2,1)S(1)} fusion(bf16[1048576]{0:T(1024)(128)(2,1)S(1)} %bitcast.110, s32[65536]{0:T(1024)S(1)} %broadcast_clamp_fusion.1), kind=kCustom, calls=%fused_computation.2.clone | custom fusion | bytes 524288 | tf_op jit(solution)/shard_map/while/body/eval_jaxpr/jit(_take)/gather | solution.py:134
  471.6 0.1 reshape.186
  471.6 402.1 %gather_fusion.1 = bf16[65536]{0:T(1024)(128)(2,1)S(1)} fusion(bf16[1048576]{0:T(1024)(128)(2,1)S(1)} %bitcast.111, s32[65536]{0:T(1024)S(1)} %broadcast_clamp_fusion.3), kind=kCustom, calls=%fused_computation.clone | custom fusion | bytes 524288 | tf_op jit(solution)/shard_map/while/body/eval_jaxpr/jit(_take)/gather | solution.py:134
  873.7 0.1 reshape.178
  873.8 402.1 %gather_fusion.2 = bf16[65536]{0:T(1024)(128)(2,1)S(1)} fusion(bf16[1048576]{0:T(1024)(128)(2,1)S(1)} %bitcast.112, s32[65536]{0:T(1024)S(1)} %broadcast_clamp_fusion.2), kind=kCustom, calls=%fused_computation.1.clone | custom fusion | bytes 524288 | tf_op jit(solution)/shard_map/while/body/eval_jaxpr/jit(_take)/gather | solution.py:134
  1275.8 0.1 reshape.182
  1275.9 0.0 copy-start.2
  1275.9 0.0 copy-start.4
  1275.9 0.0 copy-start.8
  1275.9 0.0 copy-start.9
  1275.9 0.0 copy-start.11
  1275.9 402.1 %gather_fusion.4 = bf16[65536]{0:T(1024)(128)(2,1)S(1)} fusion(bf16[1048576]{0:T(1024)(128)(2,1)S(1)} %bitcast.113, s32[65536]{0:T(1024)S(1)} %broadcast_clamp_fusion), kind=kCustom, calls=%fused_computation.3.clone | custom fusion | bytes 524288 | tf_op jit(solution)/shard_map/while/body/eval_jaxpr/jit(_take)/gather | solution.py:134
  1678.0 0.1 reshape.190
  1678.1 2.0 fusion.38
  1680.2 0.0 reduce-scatter.2.cloned.1.call-update
  1680.2 15.9 reduce-scatter.2.cloned.1.call-done
  (18 shorter events, 0.2 us)
Async XLA Ops:
  6.5 2.1 copy-start.5
  23.4 0.9 copy-start.12
  28.0 10.4 copy-start.6
  28.0 10.4 copy-start.10
  28.0 38.0 %all-to-all-start = ((bf16[1,32,4,8192]{3,2,0,1:T(4,128)(2,1)}), bf16[1,32,4,8192]{3,2,0,1:T(4,128)(2,1)S(1)}, u32[]{:S(2)}, u32[]{:S(2)}) async-start(bf16[1,32,4,8192]{3,2,0,1:T(4,128)(2,1)} %bitcast.115), calls=%async_computation | async-start | bytes 4194304 | tf_op jit(solution)/shard_map/all_to_all | solution.py:122
  37.7 1658.4 %reduce-scatter.2.cloned.1.call-start = ((), (), s32[]{:S(2)}) async-start(), calls=%async_computation.2 | async-start | bytes 327680 | tf_op jit(solution)/shard_map/reduce_scatter | solution.py:149
  39.7 0.7 copy-start.1
  39.7 0.8 copy-start.3
  39.7 0.8 copy-start.7
  66.0 1.3 copy-start
  1275.9 402.2 %copy-start.2 = (s32[16,4096]{1,0:T(8,128)S(1)}, s32[16,4096]{1,0:T(8,128)}, u32[]{:S(2)}) copy-start(s32[16,4096]{1,0:T(8,128)} %copy-done.1) | copy-start | bytes 786436
  1275.9 402.2 %copy-start.4 = (s32[16,4096]{1,0:T(8,128)S(1)}, s32[16,4096]{1,0:T(8,128)}, u32[]{:S(2)}) copy-start(s32[16,4096]{1,0:T(8,128)} %copy-done.3) | copy-start | bytes 786436
  1275.9 402.2 %copy-start.8 = (f32[1,4096]{1,0:T(1,128)S(1)}, f32[1,4096]{1,0:T(1,128)}, u32[]{:S(2)}) copy-start(f32[1,4096]{1,0:T(1,128)} %param.14) | copy-start | bytes 49156
  1275.9 402.2 %copy-start.9 = (f32[1,4096]{1,0:T(1,128)S(1)}, f32[1,4096]{1,0:T(1,128)}, u32[]{:S(2)}) copy-start(f32[1,4096]{1,0:T(1,128)} %broadcast_subtract_fusion) | copy-start | bytes 49156
  1275.9 402.2 %copy-start.11 = (f32[1,4096]{1,0:T(1,128)S(1)}, f32[1,4096]{1,0:T(1,128)}, u32[]{:S(2)}) copy-start(f32[1,4096]{1,0:T(1,128)} %param.15) | copy-start | bytes 49156
Sparse Core Ops, SparseCore 0:
  1680.3 15.7 reduce-scatter.1
where the time goes:
time: 1700 us
  local copies, waits for them, and re-layouts  1620 us (95%)
  waiting for transfers between devices  40.8 us (2%)
    gather x8, local copies, waits for them, and re-layouts, fetch(): return jnp.take(flat, index).astype(jnp.float32)  1610 us
  transfers between devices with their start and end apart: 2, of which 2 were waited for; matrix products, arithmetic and copies ran while one was open for 0% of the time, Pallas kernels for 0%

commit v1 on v0

v1 whole, which is shorter than its diff:
```python
import math

import jax
import jax.numpy as jnp
from jax import lax
from jax.experimental import pallas as pl
from jax.experimental.pallas import tpu as pltpu
from jax.sharding import PartitionSpec as P

F32 = jnp.float32
BF16 = jnp.bfloat16
I32 = jnp.int32
MESH = pl.DeviceIdType.MESH

ANGLES = 4
SLABS = 32
BANDS = 4
BAND = 4
ROWS = 16
COLS = 8192
DET = 512
PLANES = 16
VOX = 4096
OUT_VOX = 1024
SUB = 256
BLOCKS = 16
HALF = COLS // 2
TOEP_LO = -(BLOCKS - 1) * SUB - 128
TOEP_WIDTH = (2 * BLOCKS - 1) * SUB + 128
TILE = 512


def split_hi_lo(value):
    high = value.astype(BF16)
    low = (value - high.astype(F32)).astype(BF16)
    return high, low


def ramp_odd(offset):
    step = (2 * offset - 1).astype(F32)
    return (-1.0 / math.pi**2) / (step * step)


def make_toeplitz(toep_hi, toep_lo):
    lane = lax.broadcasted_iota(I32, (128, 128), 1)
    sub = lax.broadcasted_iota(I32, (128, 128), 0)
    base = lane - sub + TOEP_LO

    def one(j, carry):
        high, low = split_hi_lo(ramp_odd(base + j * 128))
        where = pl.ds(pl.multiple_of(j * 128, 128), 128)
        toep_hi[:, where] = high
        toep_lo[:, where] = low
        return carry

    lax.fori_loop(0, TOEP_WIDTH // 128, one, 0)


def load_weighted(slab, x_ref, xs_hi, xs_lo):
    scale = 2.0 * COLS
    row = lax.broadcasted_iota(I32, (ROWS, SUB), 0)
    lane = lax.broadcasted_iota(I32, (ROWS, SUB), 1)
    det = ((row // BAND) * SLABS + slab) * BAND + row % BAND
    down = det.astype(F32) - (DET - 1) / 2.0
    rest = scale * scale + down * down
    for kb in range(COLS // SUB):
        across = (lane + kb * SUB).astype(F32) - (COLS - 1) / 2.0
        raw = jnp.concatenate(
            [x_ref[b, :, kb * SUB : (kb + 1) * SUB] for b in range(BANDS)], axis=0
        )
        high, low = split_hi_lo(raw * (scale / jnp.sqrt(rest + across * across)))
        xs_hi[kb * ROWS : (kb + 1) * ROWS, :] = high
        xs_lo[kb * ROWS : (kb + 1) * ROWS, :] = low
    xs_hi[2 * SUB :, :] = jnp.zeros((ROWS, SUB), BF16)
    xs_lo[2 * SUB :, :] = jnp.zeros((ROWS, SUB), BF16)


def one_hot(mask):
    return jnp.where(mask, 1.0, 0.0).astype(BF16)


def split_parity(xs_hi, xs_lo, z_hi, z_lo, y_ref):
    k = lax.broadcasted_iota(I32, (SUB, SUB), 0)
    n = lax.broadcasted_iota(I32, (SUB, SUB), 1)
    even_odd = one_hot(k == jnp.where(n < 128, 2 * n, 2 * n - 255))
    k2 = lax.broadcasted_iota(I32, (2 * SUB, 128), 0)
    n2 = lax.broadcasted_iota(I32, (2 * SUB, 128), 1)
    later = one_hot(k2 == 2 * n2 + 2)
    first = None
    quarter = None
    for xs, z in ((xs_hi, z_hi), (xs_lo, z_lo)):
        here = xs[: 2 * SUB, :]
        both = jnp.concatenate([here, xs[ROWS : 2 * SUB + ROWS, :]], axis=1)
        eo = jnp.dot(here, even_odd, preferred_element_type=F32)
        es = jnp.dot(both, later, preferred_element_type=F32).astype(BF16)
        eo_b = eo[:, 128:].astype(BF16)
        for kb in range(2 * BLOCKS):
            mb, half = kb // 2, kb % 2
            lanes = slice(half * 128, half * 128 + 128)
            src = slice(kb * ROWS, (kb + 1) * ROWS)
            z[mb * 32 : mb * 32 + 16, lanes] = eo_b[src]
            z[mb * 32 + 16 : mb * 32 + 32, lanes] = es[src]
        quarter = eo if quarter is None else quarter + eo
        first = eo[:ROWS, 0:1] if first is None else first + eo[:ROWS, 0:1]
    quarter = quarter * 0.25
    lane = lax.broadcasted_iota(I32, (ROWS, 128), 1)
    for kb in range(2 * BLOCKS):
        mb, half = kb // 2, kb % 2
        lanes = slice(half * 128, half * 128 + 128)
        src = slice(kb * ROWS, (kb + 1) * ROWS)
        y_ref[mb * 32 : mb * 32 + 16, lanes] = quarter[src, :128]
        edge = first * ramp_odd(lane + (kb * 128 + 1))
        y_ref[mb * 32 + 16 : mb * 32 + 32, lanes] = quarter[src, 128:] + edge


def convolve(toep_hi, toep_lo, z_hi, z_lo, y_ref):
    for d in range(-(BLOCKS - 1), BLOCKS):
        at = d * SUB - TOEP_LO
        count = (BLOCKS - abs(d)) * 32
        src = slice(max(0, -d) * 32, max(0, -d) * 32 + count)
        dst = slice(max(0, d) * 32, max(0, d) * 32 + count)
        t_hi = jnp.concatenate(
            [toep_hi[:, at : at + SUB], toep_hi[:, at - 128 : at + 128]], axis=0
        )
        t_lo = jnp.concatenate(
            [toep_lo[:, at : at + SUB], toep_lo[:, at - 128 : at + 128]], axis=0
        )
        part = (
            jnp.dot(z_hi[src, :], t_hi, preferred_element_type=F32)
            + jnp.dot(z_lo[src, :], t_hi, preferred_element_type=F32)
            + jnp.dot(z_hi[src, :], t_lo, preferred_element_type=F32)
        )
        y_ref[dst, :] += part


def round_filtered(y_ref, f_even, f_odd):
    for mb in range(BLOCKS):
        f_even[mb * 16 : mb * 16 + 16, :] = y_ref[mb * 32 : mb * 32 + 16, :].astype(BF16)
        f_odd[mb * 16 : mb * 16 + 16, :] = y_ref[mb * 32 + 16 : mb * 32 + 32, :].astype(BF16)


def pick_columns(f_ref, index):
    low = jnp.bitwise_and(index, SUB - 1)
    high = lax.shift_right_logical(index, 8)
    row = lax.broadcasted_iota(I32, (SUB, TILE), 0)
    hot = one_hot(row == low)
    wide = jnp.dot(f_ref[...], hot, preferred_element_type=F32)
    high16 = jnp.broadcast_to(high, (ROWS, TILE))
    got = wide[:ROWS]
    for mb in range(1, BLOCKS):
        got = jnp.where(high16 == mb, wide[mb * ROWS : (mb + 1) * ROWS], got)
    return got


def interpolate_columns(at, f_even, f_odd, c_ref, b_ref, w_ref):
    where = pl.ds(at, TILE)
    column = c_ref[:, where]
    frac = b_ref[:, where]
    weight = w_ref[:, where]
    odd = jnp.bitwise_and(column, 1) == 1
    even_weight = jnp.where(odd, frac, 1.0 - frac) * weight
    odd_weight = jnp.where(odd, 1.0 - frac, frac) * weight
    even_part = pick_columns(f_even, lax.shift_right_logical(column + 1, 1))
    odd_part = pick_columns(f_odd, lax.shift_right_logical(column, 1))
    return even_part * even_weight + odd_part * odd_weight


def kernel(
    x_hbm, start_hbm, rows_hbm, frac_hbm, col_hbm, colf_hbm, dist_hbm, out_ref,
    x_v, start_v, rows_v, frac_v, col_v, colf_v, dist_v,
    toep_hi, toep_lo, xs_hi, xs_lo, z_hi, z_lo, y_ref, f_even, f_odd,
    s_send, s_recv, h_send, h_recv, o_send, o_recv, st_ref,
    in_sem, s_ssem, s_rsem, h_ssem, h_rsem, o_ssem, o_rsem,
):
    angle = lax.axis_index("angle")
    slab = lax.axis_index("slab")
    owner = slab // 8
    seat = slab % 8
    at_home = owner == angle

    barrier = pltpu.get_barrier_semaphore()

    def greet_slab(o, carry):
        pl.semaphore_signal(
            barrier, inc=1, device_id=(angle, lax.rem(slab + o, SLABS)), device_id_type=MESH
        )
        return carry

    lax.fori_loop(1, SLABS, greet_slab, 0)

    def greet_sender(o, carry):
        other_angle = o // 8
        other_slab = angle * 8 + o % 8
        mine = jnp.logical_and(other_angle == angle, other_slab == slab)

        @pl.when(jnp.logical_not(mine))
        def _():
            pl.semaphore_signal(
                barrier, inc=1, device_id=(other_angle, other_slab), device_id_type=MESH
            )

        return carry

    lax.fori_loop(0, 32, greet_sender, 0)

    loads = [
        pltpu.make_async_copy(src, dst, in_sem.at[i])
        for i, (src, dst) in enumerate(
            (
                (start_hbm, start_v),
                (rows_hbm, rows_v),
                (frac_hbm, frac_v),
                (x_hbm, x_v),
                (col_hbm, col_v),
                (colf_hbm, colf_v),
                (dist_hbm, dist_v),
            )
        )
    ]
    for load in loads:
        load.start()

    for load in loads[:3]:
        load.wait()
    lane32 = lax.broadcasted_iota(I32, (1, SLABS), 1)
    first_row = BAND * jnp.sum(jnp.where(lane32 == slab, start_v[...], 0), axis=1, keepdims=True)
    for t in range(SLABS):
        lanes = slice(t * 128, t * 128 + 128)
        s_send[t] = (rows_v[:, lanes] + first_row).astype(F32) + frac_v[:, lanes]

    @pl.when(at_home)
    def _():
        pl.semaphore_wait(barrier, 62)

    @pl.when(jnp.logical_not(at_home))
    def _():
        pl.semaphore_wait(barrier, 63)

    def send_rows(o, carry):
        peer = lax.rem(slab + o, SLABS)
        pltpu.make_async_remote_copy(
            src_ref=s_send.at[peer], dst_ref=s_recv.at[slab],
            send_sem=s_ssem, recv_sem=s_rsem,
            device_id=(angle, peer), device_id_type=MESH,
        ).start()
        return carry

    lax.fori_loop(1, SLABS, send_rows, 0)
    s_recv[slab] = s_send[slab]

    make_toeplitz(toep_hi, toep_lo)
    for load in loads[3:]:
        load.wait()
    load_weighted(slab, x_v, xs_hi, xs_lo)
    split_parity(xs_hi, xs_lo, z_hi, z_lo, y_ref)
    convolve(toep_hi, toep_lo, z_hi, z_lo, y_ref)
    round_filtered(y_ref, f_even, f_odd)

    def columns(i, carry):
        at = pl.multiple_of(i * TILE, TILE)
        value = interpolate_columns(at, f_even, f_odd, col_v, colf_v, dist_v).astype(BF16)
        for j in range(TILE // 128):
            h_send[i * (TILE // 128) + j] = value[:, j * 128 : (j + 1) * 128]
        return carry

    lax.fori_loop(0, VOX // TILE, columns, 0)

    def send_columns(o, carry):
        peer = lax.rem(slab + o, SLABS)
        pltpu.make_async_remote_copy(
            src_ref=h_send.at[peer], dst_ref=h_recv.at[slab],
            send_sem=h_ssem, recv_sem=h_rsem,
            device_id=(angle, peer), device_id_type=MESH,
        ).start()
        return carry

    lax.fori_loop(1, SLABS, send_columns, 0)
    h_recv[slab] = h_send[slab]

    def wait_bytes(ref, count, sem):
        pltpu.make_async_copy(ref.at[pl.ds(0, count)], ref.at[pl.ds(0, count)], sem).wait()

    wait_bytes(s_recv, SLABS - 1, s_rsem)
    for g in range(4):
        st_ref[:, g * 128 : (g + 1) * 128] = (
            s_recv[g * 8 : (g + 1) * 8].reshape(128, 128).T
        )

    wait_bytes(h_recv, SLABS - 1, h_rsem)
    tables = [
        h_recv[g * 8 : (g + 1) * 8].reshape(128, 128).astype(F32).T for g in range(4)
    ]
    for g in range(4):
        pieces = []
        for v in range(16):
            position = st_ref[v * 8 : v * 8 + 8, g * 128 : (g + 1) * 128]
            row = position.astype(I32)
            frac = position - row.astype(F32)
            values = []
            for r in (row, jnp.minimum(row + 1, DET - 1)):
                lane = (
                    jnp.bitwise_and(lax.shift_right_logical(r, 2), 7) * 16
                    + lax.shift_right_logical(r, 7) * 4
                    + jnp.bitwise_and(r, 3)
                )
                which = jnp.bitwise_and(lax.shift_right_logical(r, 5), 3)
                got = None
                for k in range(4):
                    part = jnp.take_along_axis(
                        tables[k][v * 8 : v * 8 + 8], lane, axis=1, mode="promise_in_bounds"
                    )
                    got = part if got is None else jnp.where(which == k, part, got)
                values.append(got)
            pieces.append((1.0 - frac) * values[0] + frac * values[1])
        o_send[g * 8 : (g + 1) * 8] = jnp.concatenate(pieces, axis=0).T.reshape(8, 16, 128)

    slot = angle * 8 + seat

    def send_planes(o, carry):
        t = lax.rem(slab + o, SLABS)
        mine = jnp.logical_and(at_home, o == 0)

        @pl.when(jnp.logical_not(mine))
        def _():
            pltpu.make_async_remote_copy(
                src_ref=o_send.at[t], dst_ref=o_recv.at[slot],
                send_sem=o_ssem, recv_sem=o_rsem,
                device_id=(owner, t), device_id_type=MESH,
            ).start()

        return carry

    lax.fori_loop(0, SLABS, send_planes, 0)

    @pl.when(at_home)
    def _():
        o_recv[slot] = o_send[slab]
        wait_bytes(o_recv, 31, o_rsem)

    @pl.when(jnp.logical_not(at_home))
    def _():
        wait_bytes(o_recv, 32, o_rsem)

    for k in range(8):
        out_ref[:, k * 128 : (k + 1) * 128] = (
            o_recv[k] + o_recv[8 + k] + o_recv[16 + k] + o_recv[24 + k]
        )

    wait_bytes(s_send, SLABS - 1, s_ssem)
    wait_bytes(h_send, SLABS - 1, h_ssem)

    @pl.when(at_home)
    def _():
        wait_bytes(o_send, 31, o_ssem)

    @pl.when(jnp.logical_not(at_home))
    def _():
        wait_bytes(o_send, 32, o_ssem)


SCRATCH = [
    pltpu.VMEM((BANDS, BAND, COLS), F32),
    pltpu.VMEM((1, SLABS), I32),
    pltpu.VMEM((PLANES, VOX), I32),
    pltpu.VMEM((PLANES, VOX), F32),
    pltpu.VMEM((1, VOX), I32),
    pltpu.VMEM((1, VOX), F32),
    pltpu.VMEM((1, VOX), F32),
    pltpu.VMEM((128, TOEP_WIDTH), BF16),
    pltpu.VMEM((128, TOEP_WIDTH), BF16),
    pltpu.VMEM((2 * SUB + ROWS, SUB), BF16),
    pltpu.VMEM((2 * SUB + ROWS, SUB), BF16),
    pltpu.VMEM((2 * SUB, SUB), BF16),
    pltpu.VMEM((2 * SUB, SUB), BF16),
    pltpu.VMEM((2 * SUB, SUB), F32),
    pltpu.VMEM((SUB, SUB), BF16),
    pltpu.VMEM((SUB, SUB), BF16),
    pltpu.VMEM((SLABS, PLANES, 128), F32),
    pltpu.VMEM((SLABS, PLANES, 128), F32),
    pltpu.VMEM((SLABS, ROWS, 128), BF16),
    pltpu.VMEM((SLABS, ROWS, 128), BF16),
    pltpu.VMEM((SLABS, PLANES, 128), F32),
    pltpu.VMEM((SLABS, PLANES, 128), F32),
    pltpu.VMEM((128, SLABS * PLANES), F32),
    pltpu.SemaphoreType.DMA((7,)),
    pltpu.SemaphoreType.DMA,
    pltpu.SemaphoreType.DMA,
    pltpu.SemaphoreType.DMA,
    pltpu.SemaphoreType.DMA,
    pltpu.SemaphoreType.DMA,
    pltpu.SemaphoreType.DMA,
]


def body(projections, band_start, row_index, row_frac, col_index, col_frac, distance_weight):
    call = pl.pallas_call(
        kernel,
        out_shape=jax.ShapeDtypeStruct((PLANES, OUT_VOX), F32),
        in_specs=[pl.BlockSpec(memory_space=pl.ANY)] * 7,
        out_specs=pl.BlockSpec(memory_space=pltpu.VMEM),
        scratch_shapes=SCRATCH,
        compiler_params=pltpu.CompilerParams(
            collective_id=0, has_side_effects=True, vmem_limit_bytes=40 * 1024 * 1024
        ),
        cost_estimate=pl.CostEstimate(
            flops=6 * 10**9, bytes_accessed=2 * 10**6, transcendentals=0
        ),
    )
    return call(
        projections.reshape(BANDS, BAND, COLS),
        band_start,
        row_index.reshape(PLANES, VOX),
        row_frac.reshape(PLANES, VOX),
        col_index,
        col_frac,
        distance_weight,
    )


def solution(mesh):
    in_specs = (
        P("angle", None, "slab", None, None),
        P("angle", None),
        P("angle", "slab", None),
        P("angle", "slab", None),
        P("angle", None),
        P("angle", None),
        P("angle", None),
    )
    out_specs = P("slab", "angle")
    return jax.shard_map(body, mesh=mesh, in_specs=in_specs, out_specs=out_specs, check_vma=False)
```

time: 1700 us -> 47.1 us (0.03)
  local copies, waits for them, and re-layouts: 1620 us -> 6.38 us
  waiting for transfers between devices: 40.8 us -> 0 us
  Pallas kernels: 0 us -> 40.3 us
    gather x10 -> x0, local copies, waits for them, and re-layouts: 1610 us -> none  [the longest x8 1610 us: fetch(): return jnp.take(flat, index).astype(jnp.float32)]
    pallas_call x0 -> x1, Pallas kernels: none -> 40.3 us  [body(): call(projections.reshape(BANDS, BAND, COLS), band_start, row_index.reshap...]
    all_to_all x1 -> x0, waiting for transfers between devices: 24.8 us -> none  [body(): lax.all_to_all(outgoing, 'slab', split_axis=1, concat_axis=1, tiled=True)]
  transfers between devices with their start and end apart: 2 -> 0, of which waited for: 2 -> 0; matrix products, arithmetic and copies ran while one was open for 0% -> 0% of each run, Pallas kernels for 0% -> 0%
where the time goes in v1:
time: 47.1 us; the launch traced here: 46.7 us
  Pallas kernels  40.3 us (86%)
  local copies, waits for them, and re-layouts  6.38 us (14%)
    pallas_call x1, Pallas kernels, body(): call(projections.reshape(BANDS, BAND, COLS), band_start, row_index.reshap...  40.3 us
    unnamed x15, local copies, waits for them, and re-layouts  6.38 us

profile of v1, /device:TPU:1, one launch (start us, length us, event | category | flops | bytes accessed | tf_op | source)
XLA Modules:
  0.0 46.7 jit_solution(14557058826793154101)
XLA Ops:
  0.0 0.0 copy-start.6
  0.0 0.7 %copy-done.6 = s32[1,32]{1,0:T(1,128)S(1)} copy-done((s32[1,32]{1,0:T(1,128)S(1)}, s32[1,32]{1,0:T(1,128)}, u32[]{:S(2)}) %copy-start.6) | copy-done | bytes 152
  0.7 0.0 copy-start
  0.7 1.0 %copy-done = f32[1,4,1,4,8192]{4,3,2,1,0:T(4,128)S(1)} copy-done((f32[1,4,1,4,8192]{4,3,2,1,0:T(4,128)S(1)}, f32[1,4,1,4,8192]{4,3,2,1,0:T(4,128)}, u32[]{:S(2)}) %copy-start) | copy-done | bytes 524312
  1.7 0.0 copy-start.1
  1.7 0.9 %copy-done.1 = s32[1,16,4096]{2,1,0:T(8,128)S(1)} copy-done((s32[1,16,4096]{2,1,0:T(8,128)S(1)}, s32[1,16,4096]{2,1,0:T(8,128)}, u32[]{:S(2)}) %copy-start.1) | copy-done | bytes 262168
  2.6 0.0 copy-start.2
  2.7 0.9 %copy-done.2 = f32[1,16,4096]{2,1,0:T(8,128)S(1)} copy-done((f32[1,16,4096]{2,1,0:T(8,128)S(1)}, f32[1,16,4096]{2,1,0:T(8,128)}, u32[]{:S(2)}) %copy-start.2) | copy-done | bytes 262168
  3.6 0.0 copy-start.3
  3.6 0.7 %copy-done.3 = s32[1,4096]{1,0:T(1,128)S(1)} copy-done((s32[1,4096]{1,0:T(1,128)S(1)}, s32[1,4096]{1,0:T(1,128)}, u32[]{:S(2)}) %copy-start.3) | copy-done | bytes 16408
  4.3 0.0 copy-start.4
  4.3 0.7 %copy-done.4 = f32[1,4096]{1,0:T(1,128)S(1)} copy-done((f32[1,4096]{1,0:T(1,128)S(1)}, f32[1,4096]{1,0:T(1,128)}, u32[]{:S(2)}) %copy-start.4) | copy-done | bytes 16408
  5.0 0.0 copy-start.5
  5.0 0.7 %copy-done.5 = f32[1,4096]{1,0:T(1,128)S(1)} copy-done((f32[1,4096]{1,0:T(1,128)S(1)}, f32[1,4096]{1,0:T(1,128)}, u32[]{:S(2)}) %copy-start.5) | copy-done | bytes 16408
  5.8 40.3 %shard_map.73 = f32[16,1024]{1,0:T(8,128)S(1)} custom-call(f32[4,4,8192]{2,1,0:T(4,128)S(1)} %bitcast.3, s32[1,32]{1,0:T(1,128)S(1)} %copy-done.6, s32[16,4096]{1,0:T(8,128)S(1)} %bitcast.4, f32[16,4096]{1,0:T(8,128)S(1)} %bitcast.5, s32[1,4096]{1,0:T(1,128)S(1)} %copy-done.3, f32[1,4096]{1,0:T(1,128)S(1)} %copy-done.4, f32[1,4096]{1,0:T(1,128)S(1)} %copy-done.5), custom_call_target="tpu_custom_call" | custom-call | flops 6000000000 | bytes 2000000 | tf_op jit(solution)/shard_map/pallas_call | solution.py:409
  46.1 0.6 %copy.9 = f32[16,1024]{1,0:T(8,128)} copy(f32[16,1024]{1,0:T(8,128)S(1)} %shard_map.73) | data formatting | bytes 131072
Async XLA Ops:
  0.0 0.7 %copy-start.6 = (s32[1,32]{1,0:T(1,128)S(1)}, s32[1,32]{1,0:T(1,128)}, u32[]{:S(2)}) copy-start(s32[1,32]{1,0:T(1,128)} %start_hbm.1) | copy-start | bytes 388
  0.7 1.0 %copy-start = (f32[1,4,1,4,8192]{4,3,2,1,0:T(4,128)S(1)}, f32[1,4,1,4,8192]{4,3,2,1,0:T(4,128)}, u32[]{:S(2)}) copy-start(f32[1,4,1,4,8192]{4,3,2,1,0:T(4,128)} %param.7) | copy-start | bytes 1572868
  1.7 0.9 %copy-start.1 = (s32[1,16,4096]{2,1,0:T(8,128)S(1)}, s32[1,16,4096]{2,1,0:T(8,128)}, u32[]{:S(2)}) copy-start(s32[1,16,4096]{2,1,0:T(8,128)} %param.9) | copy-start | bytes 786436
  2.6 0.9 %copy-start.2 = (f32[1,16,4096]{2,1,0:T(8,128)S(1)}, f32[1,16,4096]{2,1,0:T(8,128)}, u32[]{:S(2)}) copy-start(f32[1,16,4096]{2,1,0:T(8,128)} %param.10) | copy-start | bytes 786436
  3.6 0.7 %copy-start.3 = (s32[1,4096]{1,0:T(1,128)S(1)}, s32[1,4096]{1,0:T(1,128)}, u32[]{:S(2)}) copy-start(s32[1,4096]{1,0:T(1,128)} %col_hbm.1) | copy-start | bytes 49156
  4.3 0.7 %copy-start.4 = (f32[1,4096]{1,0:T(1,128)S(1)}, f32[1,4096]{1,0:T(1,128)}, u32[]{:S(2)}) copy-start(f32[1,4096]{1,0:T(1,128)} %colf_hbm.1) | copy-start | bytes 49156
  5.0 0.7 %copy-start.5 = (f32[1,4096]{1,0:T(1,128)S(1)}, f32[1,4096]{1,0:T(1,128)}, u32[]{:S(2)}) copy-start(f32[1,4096]{1,0:T(1,128)} %dist_hbm.1) | copy-start | bytes 49156

commit v2 on v1

--- a/solution.py
+++ b/solution.py
@@ -13,6 +13,7 @@
 MESH = pl.DeviceIdType.MESH
 
 ANGLES = 4
+OWNERS = 4
 SLABS = 32
 BANDS = 4
 BAND = 4
@@ -165,18 +166,101 @@
     return even_part * even_weight + odd_part * odd_weight
 
 
+def pair_halves(read, k, core):
+    first = core * OUT_VOX + k * 64
+    second = first + 2 * OUT_VOX
+    return jnp.concatenate([read(first), read(second)], axis=1)
+
+
+def deal_columns(src, dst):
+    for s in range(SLABS):
+        dst[:, s * 128 : (s + 1) * 128] = pair_halves(
+            lambda at: src[:, at : at + 64], s // 2, s % 2
+        )
+
+
+def deal_rows(slab, start_v, rows_v, frac_v, s_send):
+    lane = lax.broadcasted_iota(I32, (1, SLABS), 1)
+    first_row = BAND * jnp.sum(jnp.where(lane == slab, start_v[...], 0), axis=1, keepdims=True)
+    for q in range(OWNERS):
+        lanes = slice(q * OUT_VOX, (q + 1) * OUT_VOX)
+        position = (rows_v[:, lanes] + first_row).astype(F32) + frac_v[:, lanes]
+        for k in range(16):
+            half = slice((q // 2) * 64, (q // 2) * 64 + 64)
+            s_send[2 * k + q % 2, :, half] = position[:, k * 64 : k * 64 + 64]
+
+
+def transpose_rows(s_recv, st_ref):
+    for zh in range(2):
+        for th in range(2):
+            block = s_recv[th * 16 : th * 16 + 16, zh * 8 : zh * 8 + 8, :].reshape(128, 128)
+            at = (zh * 2 + th) * 128
+            st_ref[:, at : at + 128] = block.T
+
+
+def make_tables(h_recv):
+    return [h_recv[g * 8 : (g + 1) * 8].reshape(128, 128).astype(F32).T for g in range(4)]
+
+
+def look_up(position, tables, v):
+    row = position.astype(I32)
+    frac = position - row.astype(F32)
+    values = []
+    for r in (row, jnp.minimum(row + 1, DET - 1)):
+        lane = (
+            jnp.bitwise_and(lax.shift_right_logical(r, 2), 7) * 16
+            + lax.shift_right_logical(r, 7) * 4
+            + jnp.bitwise_and(r, 3)
+        )
+        which = jnp.bitwise_and(lax.shift_right_logical(r, 5), 3)
+        got = None
+        for k in range(4):
+            part = jnp.take_along_axis(
+                tables[k][v * 8 : v * 8 + 8], lane, axis=1, mode="promise_in_bounds"
+            )
+            got = part if got is None else jnp.where(which == k, part, got)
+        values.append(got)
+    return (1.0 - frac) * values[0] + frac * values[1]
+
+
+def look_up_half(th, st_ref, tables, o_send):
+    found = []
+    for zh in range(2):
+        at = (zh * 2 + th) * 128
+        found.append(
+            [look_up(st_ref[v * 8 : v * 8 + 8, at : at + 128], tables, v) for v in range(16)]
+        )
+    for e in range(2):
+        stack = jnp.concatenate(found[0][e * 8 : e * 8 + 8] + found[1][e * 8 : e * 8 + 8], axis=0)
+        o_send[e, th * 16 : th * 16 + 16] = stack.T.reshape(16, 8, 128)
+
+
+def sum_angles(o_recv, out_ref):
+    for m in range(8):
+        total = []
+        for k in (2 * m, 2 * m + 1):
+            total.append(o_recv[k] + o_recv[16 + k] + o_recv[32 + k] + o_recv[48 + k])
+        lanes = slice(m * 128, (m + 1) * 128)
+        for zh in range(2):
+            half = slice(zh * 64, zh * 64 + 64)
+            out_ref[zh * 8 : zh * 8 + 8, lanes] = jnp.concatenate(
+                [total[0][:, half], total[1][:, half]], axis=1
+            )
+
+
 def kernel(
     x_hbm, start_hbm, rows_hbm, frac_hbm, col_hbm, colf_hbm, dist_hbm, out_ref,
     x_v, start_v, rows_v, frac_v, col_v, colf_v, dist_v,
+    col_d, colf_d, dist_d,
     toep_hi, toep_lo, xs_hi, xs_lo, z_hi, z_lo, y_ref, f_even, f_odd,
     s_send, s_recv, h_send, h_recv, o_send, o_recv, st_ref,
-    in_sem, s_ssem, s_rsem, h_ssem, h_rsem, o_ssem, o_rsem,
+    in_sem, s_ssem, s_rsem, h_ssem, h_rsem, o_ssem, o_rsem, plane_sem,
 ):
     angle = lax.axis_index("angle")
     slab = lax.axis_index("slab")
-    owner = slab // 8
-    seat = slab % 8
-    at_home = owner == angle
+    chip = slab // 2
+    core = slab % 2
+    at_home = angle % 2 == core
 
     barrier = pltpu.get_barrier_semaphore()
 
@@ -187,30 +271,19 @@
         return carry
 
     lax.fori_loop(1, SLABS, greet_slab, 0)
-
-    def greet_sender(o, carry):
-        other_angle = o // 8
-        other_slab = angle * 8 + o % 8
-        mine = jnp.logical_and(other_angle == angle, other_slab == slab)
-
-        @pl.when(jnp.logical_not(mine))
-        def _():
-            pl.semaphore_signal(
-                barrier, inc=1, device_id=(other_angle, other_slab), device_id_type=MESH
-            )
-
-        return carry
-
-    lax.fori_loop(0, 32, greet_sender, 0)
+    for o in range(1, ANGLES):
+        pl.semaphore_signal(
+            barrier, inc=1, device_id=(lax.rem(angle + o, ANGLES), slab), device_id_type=MESH
+        )
 
     loads = [
         pltpu.make_async_copy(src, dst, in_sem.at[i])
         for i, (src, dst) in enumerate(
             (
+                (x_hbm, x_v),
                 (start_hbm, start_v),
                 (rows_hbm, rows_v),
                 (frac_hbm, frac_v),
-                (x_hbm, x_v),
                 (col_hbm, col_v),
                 (colf_hbm, colf_v),
                 (dist_hbm, dist_v),
@@ -220,21 +293,22 @@
     for load in loads:
         load.start()
 
-    for load in loads[:3]:
+    make_toeplitz(toep_hi, toep_lo)
+    for load in loads:
         load.wait()
-    lane32 = lax.broadcasted_iota(I32, (1, SLABS), 1)
-    first_row = BAND * jnp.sum(jnp.where(lane32 == slab, start_v[...], 0), axis=1, keepdims=True)
-    for t in range(SLABS):
-        lanes = slice(t * 128, t * 128 + 128)
-        s_send[t] = (rows_v[:, lanes] + first_row).astype(F32) + frac_v[:, lanes]
-
-    @pl.when(at_home)
-    def _():
-        pl.semaphore_wait(barrier, 62)
-
-    @pl.when(jnp.logical_not(at_home))
-    def _():
-        pl.semaphore_wait(barrier, 63)
+    deal_rows(slab, start_v, rows_v, frac_v, s_send)
+    for src, dst in ((col_v, col_d), (colf_v, colf_d), (dist_v, dist_d)):
+        deal_columns(src, dst)
+    load_weighted(slab, x_v, xs_hi, xs_lo)
+    split_parity(xs_hi, xs_lo, z_hi, z_lo, y_ref)
+    convolve(toep_hi, toep_lo, z_hi, z_lo, y_ref)
+    round_filtered(y_ref, f_even, f_odd)
+
+    pl.semaphore_wait(barrier, SLABS - 1 + ANGLES - 1)
+    for o in range(1, ANGLES):
+        pl.semaphore_signal(
+            plane_sem, inc=1, device_id=(lax.rem(angle + o, ANGLES), slab), device_id_type=MESH
+        )
 
     def send_rows(o, carry):
         peer = lax.rem(slab + o, SLABS)
@@ -248,114 +322,80 @@
     lax.fori_loop(1, SLABS, send_rows, 0)
     s_recv[slab] = s_send[slab]
 
-    make_toeplitz(toep_hi, toep_lo)
-    for load in loads[3:]:
-        load.wait()
-    load_weighted(slab, x_v, xs_hi, xs_lo)
-    split_parity(xs_hi, xs_lo, z_hi, z_lo, y_ref)
-    convolve(toep_hi, toep_lo, z_hi, z_lo, y_ref)
-    round_filtered(y_ref, f_even, f_odd)
-
     def columns(i, carry):
-        at = pl.multiple_of(i * TILE, TILE)
-        value = interpolate_columns(at, f_even, f_odd, col_v, colf_v, dist_v).astype(BF16)
+        j = i // 2
+        turn = lax.rem(slab // 8 + 2 + j + (j // 2) * (5 - 2 * j), 4)
+        tile = turn * 2 + lax.rem(slab // 4 + 1 + i, 2)
+        at = pl.multiple_of(tile * TILE, TILE)
+        value = interpolate_columns(at, f_even, f_odd, col_d, colf_d, dist_d).astype(BF16)
         for j in range(TILE // 128):
-            h_send[i * (TILE // 128) + j] = value[:, j * 128 : (j + 1) * 128]
+            peer = tile * (TILE // 128) + j
+            h_send[peer] = value[:, j * 128 : (j + 1) * 128]
+
+            @pl.when(peer != slab)
+            def _():
+                pltpu.make_async_remote_copy(
+                    src_ref=h_send.at[peer], dst_ref=h_recv.at[slab],
+                    send_sem=h_ssem, recv_sem=h_rsem,
+                    device_id=(angle, peer), device_id_type=MESH,
+                ).start()
+
         return carry
 
     lax.fori_loop(0, VOX // TILE, columns, 0)
-
-    def send_columns(o, carry):
-        peer = lax.rem(slab + o, SLABS)
-        pltpu.make_async_remote_copy(
-            src_ref=h_send.at[peer], dst_ref=h_recv.at[slab],
-            send_sem=h_ssem, recv_sem=h_rsem,
-            device_id=(angle, peer), device_id_type=MESH,
-        ).start()
-        return carry
-
-    lax.fori_loop(1, SLABS, send_columns, 0)
     h_recv[slab] = h_send[slab]
 
     def wait_bytes(ref, count, sem):
         pltpu.make_async_copy(ref.at[pl.ds(0, count)], ref.at[pl.ds(0, count)], sem).wait()
 
     wait_bytes(s_recv, SLABS - 1, s_rsem)
-    for g in range(4):
-        st_ref[:, g * 128 : (g + 1) * 128] = (
-            s_recv[g * 8 : (g + 1) * 8].reshape(128, 128).T
-        )
-
+    transpose_rows(s_recv, st_ref)
     wait_bytes(h_recv, SLABS - 1, h_rsem)
-    tables = [
-        h_recv[g * 8 : (g + 1) * 8].reshape(128, 128).astype(F32).T for g in range(4)
-    ]
-    for g in range(4):
-        pieces = []
-        for v in range(16):
-            position = st_ref[v * 8 : v * 8 + 8, g * 128 : (g + 1) * 128]
-            row = position.astype(I32)
-            frac = position - row.astype(F32)
-            values = []
-            for r in (row, jnp.minimum(row + 1, DET - 1)):
-                lane = (
-                    jnp.bitwise_and(lax.shift_right_logical(r, 2), 7) * 16
-                    + lax.shift_right_logical(r, 7) * 4
-                    + jnp.bitwise_and(r, 3)
-                )
-                which = jnp.bitwise_and(lax.shift_right_logical(r, 5), 3)
-                got = None
-                for k in range(4):
-                    part = jnp.take_along_axis(
-                        tables[k][v * 8 : v * 8 + 8], lane, axis=1, mode="promise_in_bounds"
-                    )
-                    got = part if got is None else jnp.where(which == k, part, got)
-                values.append(got)
-            pieces.append((1.0 - frac) * values[0] + frac * values[1])
-        o_send[g * 8 : (g + 1) * 8] = jnp.concatenate(pieces, axis=0).T.reshape(8, 16, 128)
-
-    slot = angle * 8 + seat
-
-    def send_planes(o, carry):
-        t = lax.rem(slab + o, SLABS)
-        mine = jnp.logical_and(at_home, o == 0)
-
-        @pl.when(jnp.logical_not(mine))
-        def _():
-            pltpu.make_async_remote_copy(
-                src_ref=o_send.at[t], dst_ref=o_recv.at[slot],
-                send_sem=o_ssem, recv_sem=o_rsem,
-                device_id=(owner, t), device_id_type=MESH,
-            ).start()
-
-        return carry
-
-    lax.fori_loop(0, SLABS, send_planes, 0)
+    tables = make_tables(h_recv)
+    pl.semaphore_wait(plane_sem, ANGLES - 1)
+
+    slot = angle * 16 + chip
+    for th in range(2):
+        look_up_half(th, st_ref, tables, o_send)
+
+        def send_planes(o, carry):
+            t = th * 16 + lax.rem(slab + o, 16)
+            for e in range(2):
+                owner = core + 2 * e
+
+                @pl.when(jnp.logical_not(jnp.logical_and(owner == angle, t == slab)))
+                def _():
+                    pltpu.make_async_remote_copy(
+                        src_ref=o_send.at[e, t], dst_ref=o_recv.at[slot],
+                        send_sem=o_ssem, recv_sem=o_rsem,
+                        device_id=(owner, t), device_id_type=MESH,
+                    ).start()
+
+            return carry
+
+        lax.fori_loop(0, 16, send_planes, 0)
 
     @pl.when(at_home)
     def _():
-        o_recv[slot] = o_send[slab]
-        wait_bytes(o_recv, 31, o_rsem)
+        o_recv[slot] = o_send[angle // 2, slab]
+        wait_bytes(o_recv, 63, o_rsem)
 
     @pl.when(jnp.logical_not(at_home))
     def _():
-        wait_bytes(o_recv, 32, o_rsem)
-
-    for k in range(8):
-        out_ref[:, k * 128 : (k + 1) * 128] = (
-            o_recv[k] + o_recv[8 + k] + o_recv[16 + k] + o_recv[24 + k]
-        )
+        wait_bytes(o_recv, 64, o_rsem)
+
+    sum_angles(o_recv, out_ref)
 
     wait_bytes(s_send, SLABS - 1, s_ssem)
     wait_bytes(h_send, SLABS - 1, h_ssem)
 
     @pl.when(at_home)
     def _():
-        wait_bytes(o_send, 31, o_ssem)
+        wait_bytes(o_recv, 63, o_ssem)
 
     @pl.when(jnp.logical_not(at_home))
     def _():
-        wait_bytes(o_send, 32, o_ssem)
+        wait_bytes(o_recv, 64, o_ssem)
 
 
 SCRATCH = [
@@ -363,6 +403,9 @@
     pltpu.VMEM((1, SLABS), I32),
     pltpu.VMEM((PLANES, VOX), I32),
     pltpu.VMEM((PLANES, VOX), F32),
+    pltpu.VMEM((1, VOX), I32),
+    pltpu.VMEM((1, VOX), F32),
+    pltpu.VMEM((1, VOX), F32),
     pltpu.VMEM((1, VOX), I32),
     pltpu.VMEM((1, VOX), F32),
     pltpu.VMEM((1, VOX), F32),
@@ -379,8 +422,8 @@
     pltpu.VMEM((SLABS, PLANES, 128), F32),
     pltpu.VMEM((SLABS, ROWS, 128), BF16),
     pltpu.VMEM((SLABS, ROWS, 128), BF16),
-    pltpu.VMEM((SLABS, PLANES, 128), F32),
-    pltpu.VMEM((SLABS, PLANES, 128), F32),
+    pltpu.VMEM((2, SLABS, 8, 128), F32),
+    pltpu.VMEM((2 * SLABS, 8, 128), F32),
     pltpu.VMEM((128, SLABS * PLANES), F32),
     pltpu.SemaphoreType.DMA((7,)),
     pltpu.SemaphoreType.DMA,
@@ -389,6 +432,7 @@
     pltpu.SemaphoreType.DMA,
     pltpu.SemaphoreType.DMA,
     pltpu.SemaphoreType.DMA,
+    pltpu.SemaphoreType.REGULAR,
 ]
 
 
@@ -396,7 +440,7 @@
     call = pl.pallas_call(
         kernel,
         out_shape=jax.ShapeDtypeStruct((PLANES, OUT_VOX), F32),
-        in_specs=[pl.BlockSpec(memory_space=pl.ANY)] * 7,
+        in_specs=[pl.BlockSpec(memory_space=pltpu.HBM)] * 7,
         out_specs=pl.BlockSpec(memory_space=pltpu.VMEM),
         scratch_shapes=SCRATCH,
         compiler_params=pltpu.CompilerParams(

time: 47.1 us -> 35 us (0.74)
  Pallas kernels: 40.3 us -> 28.2 us
    pallas_call x1, Pallas kernels: 40.3 us -> 28.2 us  [body(): call(projections.reshape(BANDS, BAND, COLS), band_start, row_index.reshap...]
where the time goes in v2:
time: 35 us; the launch traced here: 34.6 us
  Pallas kernels  28.2 us (81%)
  local copies, waits for them, and re-layouts  6.38 us (18%)
    pallas_call x1, Pallas kernels, body(): call(projections.reshape(BANDS, BAND, COLS), band_start, row_index.reshap...  28.2 us
    unnamed x15, local copies, waits for them, and re-layouts  6.38 us

profile of v2, /device:TPU:1, one launch (start us, length us, event | category | flops | bytes accessed | tf_op | source)
XLA Modules:
  0.0 34.6 jit_solution(13658095556354858634)
XLA Ops:
  0.0 0.0 copy-start.6
  0.0 0.7 %copy-done.6 = s32[1,32]{1,0:T(1,128)S(1)} copy-done((s32[1,32]{1,0:T(1,128)S(1)}, s32[1,32]{1,0:T(1,128)}, u32[]{:S(2)}) %copy-start.6) | copy-done | bytes 152
  0.7 0.0 copy-start
  0.7 1.0 %copy-done = f32[1,4,1,4,8192]{4,3,2,1,0:T(4,128)S(1)} copy-done((f32[1,4,1,4,8192]{4,3,2,1,0:T(4,128)S(1)}, f32[1,4,1,4,8192]{4,3,2,1,0:T(4,128)}, u32[]{:S(2)}) %copy-start) | copy-done | bytes 524312
  1.7 0.0 copy-start.1
  1.7 0.9 %copy-done.1 = s32[1,16,4096]{2,1,0:T(8,128)S(1)} copy-done((s32[1,16,4096]{2,1,0:T(8,128)S(1)}, s32[1,16,4096]{2,1,0:T(8,128)}, u32[]{:S(2)}) %copy-start.1) | copy-done | bytes 262168
  2.6 0.0 copy-start.2
  2.7 0.9 %copy-done.2 = f32[1,16,4096]{2,1,0:T(8,128)S(1)} copy-done((f32[1,16,4096]{2,1,0:T(8,128)S(1)}, f32[1,16,4096]{2,1,0:T(8,128)}, u32[]{:S(2)}) %copy-start.2) | copy-done | bytes 262168
  3.6 0.0 copy-start.3
  3.6 0.7 %copy-done.3 = s32[1,4096]{1,0:T(1,128)S(1)} copy-done((s32[1,4096]{1,0:T(1,128)S(1)}, s32[1,4096]{1,0:T(1,128)}, u32[]{:S(2)}) %copy-start.3) | copy-done | bytes 16408
  4.3 0.0 copy-start.4
  4.3 0.7 %copy-done.4 = f32[1,4096]{1,0:T(1,128)S(1)} copy-done((f32[1,4096]{1,0:T(1,128)S(1)}, f32[1,4096]{1,0:T(1,128)}, u32[]{:S(2)}) %copy-start.4) | copy-done | bytes 16408
  5.0 0.0 copy-start.5
  5.0 0.7 %copy-done.5 = f32[1,4096]{1,0:T(1,128)S(1)} copy-done((f32[1,4096]{1,0:T(1,128)S(1)}, f32[1,4096]{1,0:T(1,128)}, u32[]{:S(2)}) %copy-start.5) | copy-done | bytes 16408
  5.8 28.2 %shard_map.73 = f32[16,1024]{1,0:T(8,128)S(1)} custom-call(f32[4,4,8192]{2,1,0:T(4,128)S(1)} %bitcast.3, s32[1,32]{1,0:T(1,128)S(1)} %copy-done.6, s32[16,4096]{1,0:T(8,128)S(1)} %bitcast.4, f32[16,4096]{1,0:T(8,128)S(1)} %bitcast.5, s32[1,4096]{1,0:T(1,128)S(1)} %copy-done.3, f32[1,4096]{1,0:T(1,128)S(1)} %copy-done.4, f32[1,4096]{1,0:T(1,128)S(1)} %copy-done.5), custom_call_target="tpu_custom_call" | custom-call | flops 6000000000 | bytes 2000000 | tf_op jit(solution)/shard_map/pallas_call | solution.py:453
  33.9 0.6 %copy.9 = f32[16,1024]{1,0:T(8,128)} copy(f32[16,1024]{1,0:T(8,128)S(1)} %shard_map.73) | data formatting | bytes 131072
Async XLA Ops:
  0.0 0.7 %copy-start.6 = (s32[1,32]{1,0:T(1,128)S(1)}, s32[1,32]{1,0:T(1,128)}, u32[]{:S(2)}) copy-start(s32[1,32]{1,0:T(1,128)} %start_hbm.1) | copy-start | bytes 388
  0.7 1.0 %copy-start = (f32[1,4,1,4,8192]{4,3,2,1,0:T(4,128)S(1)}, f32[1,4,1,4,8192]{4,3,2,1,0:T(4,128)}, u32[]{:S(2)}) copy-start(f32[1,4,1,4,8192]{4,3,2,1,0:T(4,128)} %param.7) | copy-start | bytes 1572868
  1.7 0.9 %copy-start.1 = (s32[1,16,4096]{2,1,0:T(8,128)S(1)}, s32[1,16,4096]{2,1,0:T(8,128)}, u32[]{:S(2)}) copy-start(s32[1,16,4096]{2,1,0:T(8,128)} %param.9) | copy-start | bytes 786436
  2.6 0.9 %copy-start.2 = (f32[1,16,4096]{2,1,0:T(8,128)S(1)}, f32[1,16,4096]{2,1,0:T(8,128)}, u32[]{:S(2)}) copy-start(f32[1,16,4096]{2,1,0:T(8,128)} %param.10) | copy-start | bytes 786436
  3.6 0.7 %copy-start.3 = (s32[1,4096]{1,0:T(1,128)S(1)}, s32[1,4096]{1,0:T(1,128)}, u32[]{:S(2)}) copy-start(s32[1,4096]{1,0:T(1,128)} %col_hbm.1) | copy-start | bytes 49156
  4.3 0.7 %copy-start.4 = (f32[1,4096]{1,0:T(1,128)S(1)}, f32[1,4096]{1,0:T(1,128)}, u32[]{:S(2)}) copy-start(f32[1,4096]{1,0:T(1,128)} %colf_hbm.1) | copy-start | bytes 49156
  5.0 0.7 %copy-start.5 = (f32[1,4096]{1,0:T(1,128)S(1)}, f32[1,4096]{1,0:T(1,128)}, u32[]{:S(2)}) copy-start(f32[1,4096]{1,0:T(1,128)} %dist_hbm.1) | copy-start | bytes 49156

commit v3 on v2

--- a/solution.py
+++ b/solution.py
@@ -29,6 +29,11 @@
 TOEP_LO = -(BLOCKS - 1) * SUB - 128
 TOEP_WIDTH = (2 * BLOCKS - 1) * SUB + 128
 TILE = 512
+FAR_FIRST = sorted(
+    ((dy, dz, dc) for dy in range(4) for dz in range(4) for dc in range(2)),
+    key=lambda at: (-min(at[0], 4 - at[0]) - min(at[1], 4 - at[1]), -at[2], at[0], at[1]),
+)
+TILE_ORDER = ((2, 1), (2, 0), (1, 1), (3, 1), (1, 0), (3, 0), (0, 1), (0, 0))
 
 
 def split_hi_lo(value):
@@ -42,19 +47,39 @@
     return (-1.0 / math.pi**2) / (step * step)
 
 
-def make_toeplitz(toep_hi, toep_lo):
+def make_toeplitz(toep):
     lane = lax.broadcasted_iota(I32, (128, 128), 1)
     sub = lax.broadcasted_iota(I32, (128, 128), 0)
-    base = lane - sub + TOEP_LO
+    base = (2 * (lane - sub + TOEP_LO) - 1).astype(F32)
 
     def one(j, carry):
-        high, low = split_hi_lo(ramp_odd(base + j * 128))
-        where = pl.ds(pl.multiple_of(j * 128, 128), 128)
-        toep_hi[:, where] = high
-        toep_lo[:, where] = low
+        for i in range(3):
+            tile = j * 3 + i
+            step = base + 256.0 * tile.astype(F32)
+            square = step * step
+            guess = pltpu.reciprocal(square, approx=True)
+            guess = guess * (2.0 - square * guess)
+            high, low = split_hi_lo(guess * (-1.0 / math.pi**2))
+            where = pl.ds(pl.multiple_of(tile * 128, 128), 128)
+            toep[0, :, where] = high
+            toep[1, :, where] = low
         return carry
 
-    lax.fori_loop(0, TOEP_WIDTH // 128, one, 0)
+    lax.fori_loop(0, TOEP_WIDTH // 384, one, 0)
+
+
+def make_hot(n, col_d, hot_even, hot_odd):
+    lanes = pl.ds(pl.multiple_of(n * SUB, SUB), SUB)
+    column = col_d[:, lanes]
+    row = lax.broadcasted_iota(I32, (SUB, SUB), 0).astype(F32).astype(BF16)
+    one = jnp.ones((SUB, SUB), BF16)
+    zero = jnp.zeros((SUB, SUB), BF16)
+    for hot, index in (
+        (hot_even, lax.shift_right_logical(column + 1, 1)),
+        (hot_odd, lax.shift_right_logical(column, 1)),
+    ):
+        low = jnp.bitwise_and(index, SUB - 1).astype(F32).astype(BF16)
+        hot[:, lanes] = jnp.where(row == low, one, zero)
 
 
 def load_weighted(slab, x_ref, xs_hi, xs_lo):
@@ -80,7 +105,7 @@
     return jnp.where(mask, 1.0, 0.0).astype(BF16)
 
 
-def split_parity(xs_hi, xs_lo, z_hi, z_lo, y_ref):
+def split_parity(xs_hi, xs_lo, z_ref, y_ref):
     k = lax.broadcasted_iota(I32, (SUB, SUB), 0)
     n = lax.broadcasted_iota(I32, (SUB, SUB), 1)
     even_odd = one_hot(k == jnp.where(n < 128, 2 * n, 2 * n - 255))
@@ -89,7 +114,7 @@
     later = one_hot(k2 == 2 * n2 + 2)
     first = None
     quarter = None
-    for xs, z in ((xs_hi, z_hi), (xs_lo, z_lo)):
+    for part, xs in enumerate((xs_hi, xs_lo)):
         here = xs[: 2 * SUB, :]
         both = jnp.concatenate([here, xs[ROWS : 2 * SUB + ROWS, :]], axis=1)
         eo = jnp.dot(here, even_odd, preferred_element_type=F32)
@@ -99,8 +124,8 @@
             mb, half = kb // 2, kb % 2
             lanes = slice(half * 128, half * 128 + 128)
             src = slice(kb * ROWS, (kb + 1) * ROWS)
-            z[mb * 32 : mb * 32 + 16, lanes] = eo_b[src]
-            z[mb * 32 + 16 : mb * 32 + 32, lanes] = es[src]
+            z_ref[part, mb * 32 : mb * 32 + 16, lanes] = eo_b[src]
+            z_ref[part, mb * 32 + 16 : mb * 32 + 32, lanes] = es[src]
         quarter = eo if quarter is None else quarter + eo
         first = eo[:ROWS, 0:1] if first is None else first + eo[:ROWS, 0:1]
     quarter = quarter * 0.25
@@ -114,24 +139,25 @@
         y_ref[mb * 32 + 16 : mb * 32 + 32, lanes] = quarter[src, 128:] + edge
 
 
-def convolve(toep_hi, toep_lo, z_hi, z_lo, y_ref):
-    for d in range(-(BLOCKS - 1), BLOCKS):
-        at = d * SUB - TOEP_LO
-        count = (BLOCKS - abs(d)) * 32
-        src = slice(max(0, -d) * 32, max(0, -d) * 32 + count)
-        dst = slice(max(0, d) * 32, max(0, d) * 32 + count)
-        t_hi = jnp.concatenate(
-            [toep_hi[:, at : at + SUB], toep_hi[:, at - 128 : at + 128]], axis=0
-        )
-        t_lo = jnp.concatenate(
-            [toep_lo[:, at : at + SUB], toep_lo[:, at - 128 : at + 128]], axis=0
-        )
-        part = (
-            jnp.dot(z_hi[src, :], t_hi, preferred_element_type=F32)
-            + jnp.dot(z_lo[src, :], t_hi, preferred_element_type=F32)
-            + jnp.dot(z_hi[src, :], t_lo, preferred_element_type=F32)
-        )
-        y_ref[dst, :] += part
+def convolve(col_d, toep, hot_even, hot_odd, z_ref, y_ref):
+    def one_pass(turn, carry):
+        z_at = turn % 2
+        t_at = turn // 2
+        for n in range(2 * BLOCKS - 1):
+            d = n - (BLOCKS - 1)
+            at = n * SUB + 128
+            count = (BLOCKS - abs(d)) * 32
+            src = slice(max(0, -d) * 32, max(0, -d) * 32 + count)
+            dst = slice(max(0, d) * 32, max(0, d) * 32 + count)
+            table = jnp.concatenate(
+                [toep[t_at, :, at : at + SUB], toep[t_at, :, at - 128 : at + 128]], axis=0
+            )
+            y_ref[dst, :] += jnp.dot(z_ref[z_at, src, :], table, preferred_element_type=F32)
+            if n % 5 == 2:
+                make_hot(jnp.minimum(turn * 6 + n // 5, VOX // SUB - 1), col_d, hot_even, hot_odd)
+        return carry
+
+    lax.fori_loop(0, 3, one_pass, 0)
 
 
 def round_filtered(y_ref, f_even, f_odd):
@@ -140,20 +166,16 @@
         f_odd[mb * 16 : mb * 16 + 16, :] = y_ref[mb * 32 + 16 : mb * 32 + 32, :].astype(BF16)
 
 
-def pick_columns(f_ref, index):
-    low = jnp.bitwise_and(index, SUB - 1)
-    high = lax.shift_right_logical(index, 8)
-    row = lax.broadcasted_iota(I32, (SUB, TILE), 0)
-    hot = one_hot(row == low)
+def pick_columns(f_ref, hot, index):
+    high16 = jnp.broadcast_to(lax.shift_right_logical(index, 8), (ROWS, TILE))
     wide = jnp.dot(f_ref[...], hot, preferred_element_type=F32)
-    high16 = jnp.broadcast_to(high, (ROWS, TILE))
     got = wide[:ROWS]
     for mb in range(1, BLOCKS):
         got = jnp.where(high16 == mb, wide[mb * ROWS : (mb + 1) * ROWS], got)
     return got
 
 
-def interpolate_columns(at, f_even, f_odd, c_ref, b_ref, w_ref):
+def interpolate_columns(at, f_even, f_odd, hot_even, hot_odd, c_ref, b_ref, w_ref):
     where = pl.ds(at, TILE)
     column = c_ref[:, where]
     frac = b_ref[:, where]
@@ -161,8 +183,8 @@
     odd = jnp.bitwise_and(column, 1) == 1
     even_weight = jnp.where(odd, frac, 1.0 - frac) * weight
     odd_weight = jnp.where(odd, 1.0 - frac, frac) * weight
-    even_part = pick_columns(f_even, lax.shift_right_logical(column + 1, 1))
-    odd_part = pick_columns(f_odd, lax.shift_right_logical(column, 1))
+    even_part = pick_columns(f_even, hot_even[:, where], lax.shift_right_logical(column + 1, 1))
+    odd_part = pick_columns(f_odd, hot_odd[:, where], lax.shift_right_logical(column, 1))
     return even_part * even_weight + odd_part * odd_weight
 
 
@@ -252,7 +274,7 @@
     x_hbm, start_hbm, rows_hbm, frac_hbm, col_hbm, colf_hbm, dist_hbm, out_ref,
     x_v, start_v, rows_v, frac_v, col_v, colf_v, dist_v,
     col_d, colf_d, dist_d,
-    toep_hi, toep_lo, xs_hi, xs_lo, z_hi, z_lo, y_ref, f_even, f_odd,
+    toep, hot_even, hot_odd, xs_hi, xs_lo, z_ref, y_ref, f_even, f_odd,
     s_send, s_recv, h_send, h_recv, o_send, o_recv, st_ref,
     in_sem, s_ssem, s_rsem, h_ssem, h_rsem, o_ssem, o_rsem, plane_sem,
 ):
@@ -262,47 +284,54 @@
     core = slab % 2
     at_home = angle % 2 == core
 
-    barrier = pltpu.get_barrier_semaphore()
-
-    def greet_slab(o, carry):
-        pl.semaphore_signal(
-            barrier, inc=1, device_id=(angle, lax.rem(slab + o, SLABS)), device_id_type=MESH
-        )
-        return carry
-
-    lax.fori_loop(1, SLABS, greet_slab, 0)
-    for o in range(1, ANGLES):
-        pl.semaphore_signal(
-            barrier, inc=1, device_id=(lax.rem(angle + o, ANGLES), slab), device_id_type=MESH
-        )
+    ys = [lax.rem(slab // 8 + dy, 4) * 8 for dy in range(4)]
+    zs = [lax.rem(chip + dz, 4) * 2 for dz in range(4)]
+    cores = (core, 1 - core)
+
+    def far_first(o):
+        dy, dz, dc = FAR_FIRST[o]
+        return ys[dy] + zs[dz] + cores[dc]
 
     loads = [
         pltpu.make_async_copy(src, dst, in_sem.at[i])
         for i, (src, dst) in enumerate(
             (
                 (x_hbm, x_v),
+                (col_hbm, col_v),
+                (colf_hbm, colf_v),
+                (dist_hbm, dist_v),
                 (start_hbm, start_v),
                 (rows_hbm, rows_v),
                 (frac_hbm, frac_v),
-                (col_hbm, col_v),
-                (colf_hbm, colf_v),
-                (dist_hbm, dist_v),
             )
         )
     ]
     for load in loads:
         load.start()
 
-    make_toeplitz(toep_hi, toep_lo)
+    barrier = pltpu.get_barrier_semaphore()
+
+    def greet(o, carry):
+        pl.semaphore_signal(
+            barrier, inc=1, device_id=(angle, far_first(o)), device_id_type=MESH
+        )
+        return carry
+
+    for o in range(SLABS - 1):
+        greet(o, 0)
+    for o in range(1, ANGLES):
+        pl.semaphore_signal(
+            barrier, inc=1, device_id=(lax.rem(angle + o, ANGLES), slab), device_id_type=MESH
+        )
+
+    make_toeplitz(toep)
     for load in loads:
         load.wait()
-    deal_rows(slab, start_v, rows_v, frac_v, s_send)
     for src, dst in ((col_v, col_d), (colf_v, colf_d), (dist_v, dist_d)):
         deal_columns(src, dst)
     load_weighted(slab, x_v, xs_hi, xs_lo)
-    split_parity(xs_hi, xs_lo, z_hi, z_lo, y_ref)
-    convolve(toep_hi, toep_lo, z_hi, z_lo, y_ref)
-    round_filtered(y_ref, f_even, f_odd)
+    split_parity(xs_hi, xs_lo, z_ref, y_ref)
+    deal_rows(slab, start_v, rows_v, frac_v, s_send)
 
     pl.semaphore_wait(barrier, SLABS - 1 + ANGLES - 1)
     for o in range(1, ANGLES):
@@ -310,39 +339,36 @@
             plane_sem, inc=1, device_id=(lax.rem(angle + o, ANGLES), slab), device_id_type=MESH
         )
 
+    def send(src, dst, send_sem, recv_sem, to_angle, to_slab):
+        pltpu.make_async_remote_copy(
+            src_ref=src, dst_ref=dst, send_sem=send_sem, recv_sem=recv_sem,
+            device_id=(to_angle, to_slab), device_id_type=MESH,
+        ).start()
+
     def send_rows(o, carry):
-        peer = lax.rem(slab + o, SLABS)
-        pltpu.make_async_remote_copy(
-            src_ref=s_send.at[peer], dst_ref=s_recv.at[slab],
-            send_sem=s_ssem, recv_sem=s_rsem,
-            device_id=(angle, peer), device_id_type=MESH,
-        ).start()
+        peer = far_first(o)
+        send(s_send.at[peer], s_recv.at[slab], s_ssem, s_rsem, angle, peer)
         return carry
 
-    lax.fori_loop(1, SLABS, send_rows, 0)
+    for o in range(SLABS - 1):
+        send_rows(o, 0)
     s_recv[slab] = s_send[slab]
 
-    def columns(i, carry):
-        j = i // 2
-        turn = lax.rem(slab // 8 + 2 + j + (j // 2) * (5 - 2 * j), 4)
-        tile = turn * 2 + lax.rem(slab // 4 + 1 + i, 2)
+    convolve(col_d, toep, hot_even, hot_odd, z_ref, y_ref)
+    round_filtered(y_ref, f_even, f_odd)
+
+    for i, (dy, dz) in enumerate(TILE_ORDER):
+        tile = lax.rem(slab // 8 + dy, 4) * 2 + lax.rem(slab // 4 + dz, 2)
         at = pl.multiple_of(tile * TILE, TILE)
-        value = interpolate_columns(at, f_even, f_odd, col_d, colf_d, dist_d).astype(BF16)
-        for j in range(TILE // 128):
-            peer = tile * (TILE // 128) + j
-            h_send[peer] = value[:, j * 128 : (j + 1) * 128]
-
-            @pl.when(peer != slab)
-            def _():
-                pltpu.make_async_remote_copy(
-                    src_ref=h_send.at[peer], dst_ref=h_recv.at[slab],
-                    send_sem=h_ssem, recv_sem=h_rsem,
-                    device_id=(angle, peer), device_id_type=MESH,
-                ).start()
-
-        return carry
-
-    lax.fori_loop(0, VOX // TILE, columns, 0)
+        value = interpolate_columns(
+            at, f_even, f_odd, hot_even, hot_odd, col_d, colf_d, dist_d
+        ).astype(BF16)
+        for j in range(4):
+            h_send[tile * 4 + j] = value[:, j * 128 : (j + 1) * 128]
+        for j in range(4):
+            peer = tile * 4 + lax.rem(slab + j, 4)
+            if i < len(TILE_ORDER) - 1 or j > 0:
+                send(h_send.at[peer], h_recv.at[slab], h_ssem, h_rsem, angle, peer)
     h_recv[slab] = h_send[slab]
 
     def wait_bytes(ref, count, sem):
@@ -350,30 +376,27 @@
 
     wait_bytes(s_recv, SLABS - 1, s_rsem)
     transpose_rows(s_recv, st_ref)
+    pl.semaphore_wait(plane_sem, ANGLES - 1)
     wait_bytes(h_recv, SLABS - 1, h_rsem)
     tables = make_tables(h_recv)
-    pl.semaphore_wait(plane_sem, ANGLES - 1)
-
-    slot = angle * 16 + chip
     for th in range(2):
         look_up_half(th, st_ref, tables, o_send)
 
-        def send_planes(o, carry):
-            t = th * 16 + lax.rem(slab + o, 16)
-            for e in range(2):
-                owner = core + 2 * e
-
-                @pl.when(jnp.logical_not(jnp.logical_and(owner == angle, t == slab)))
-                def _():
-                    pltpu.make_async_remote_copy(
-                        src_ref=o_send.at[e, t], dst_ref=o_recv.at[slot],
-                        send_sem=o_ssem, recv_sem=o_rsem,
-                        device_id=(owner, t), device_id_type=MESH,
-                    ).start()
-
-            return carry
-
-        lax.fori_loop(0, 16, send_planes, 0)
+    slot = angle * 16 + chip
+
+    def send_planes(o, carry):
+        t = far_first(o)
+        for e in range(2):
+            send(o_send.at[e, t], o_recv.at[slot], o_ssem, o_rsem, core + 2 * e, t)
+        return carry
+
+    for o in range(SLABS - 1):
+        send_planes(o, 0)
+    for e in range(2):
+
+        @pl.when(core + 2 * e != angle)
+        def _():
+            send(o_send.at[e, slab], o_recv.at[slot], o_ssem, o_rsem, core + 2 * e, slab)
 
     @pl.when(at_home)
     def _():
@@ -409,12 +432,12 @@
     pltpu.VMEM((1, VOX), I32),
     pltpu.VMEM((1, VOX), F32),
     pltpu.VMEM((1, VOX), F32),
-    pltpu.VMEM((128, TOEP_WIDTH), BF16),
-    pltpu.VMEM((128, TOEP_WIDTH), BF16),
+    pltpu.VMEM((2, 128, TOEP_WIDTH), BF16),
+    pltpu.VMEM((SUB, VOX), BF16),
+    pltpu.VMEM((SUB, VOX), BF16),
     pltpu.VMEM((2 * SUB + ROWS, SUB), BF16),
     pltpu.VMEM((2 * SUB + ROWS, SUB), BF16),
-    pltpu.VMEM((2 * SUB, SUB), BF16),
-    pltpu.VMEM((2 * SUB, SUB), BF16),
+    pltpu.VMEM((2, 2 * SUB, SUB), BF16),
     pltpu.VMEM((2 * SUB, SUB), F32),
     pltpu.VMEM((SUB, SUB), BF16),
     pltpu.VMEM((SUB, SUB), BF16),
@@ -450,7 +473,7 @@
             flops=6 * 10**9, bytes_accessed=2 * 10**6, transcendentals=0
         ),
     )
-    return call(
+    operands = (
         projections.reshape(BANDS, BAND, COLS),
         band_start,
         row_index.reshape(PLANES, VOX),
@@ -459,6 +482,7 @@
         col_frac,
         distance_weight,
     )
+    return call(*(pltpu.with_memory_space_constraint(value, pltpu.HBM) for value in operands))
 
 
 def solution(mesh):

time: 35 us -> 27.5 us (0.79)
  local copies, waits for them, and re-layouts: 6.38 us -> 0.63 us
  Pallas kernels: 28.2 us -> 26.7 us
    unnamed x15 -> x1, local copies, waits for them, and re-layouts: 6.38 us -> 0.63 us
    pallas_call x1, Pallas kernels: 28.2 us -> 26.7 us  [body(): call(*(pltpu.with_memory_space_constraint(value, pltpu.HBM) for value in...]
where the time goes in v3:
time: 27.5 us; the launch traced here: 27.4 us
  Pallas kernels  26.7 us (97%)
  local copies, waits for them, and re-layouts  0.63 us (2%)
    pallas_call x1, Pallas kernels, body(): call(*(pltpu.with_memory_space_constraint(value, pltpu.HBM) for value in...  26.7 us
    unnamed x1, local copies, waits for them, and re-layouts  0.63 us

profile of v3, /device:TPU:1, one launch (start us, length us, event | category | flops | bytes accessed | tf_op | source)
XLA Modules:
  0.0 27.4 jit_solution(10764141113707911713)
XLA Ops:
  0.0 26.7 %shard_map.73 = f32[16,1024]{1,0:T(8,128)S(1)} custom-call(f32[4,4,8192]{2,1,0:T(4,128)} %bitcast.3, s32[1,32]{1,0:T(1,128)} %start_hbm.1, s32[16,4096]{1,0:T(8,128)} %bitcast.4, f32[16,4096]{1,0:T(8,128)} %bitcast.5, s32[1,4096]{1,0:T(1,128)} %col_hbm.1, f32[1,4096]{1,0:T(1,128)} %colf_hbm.1, f32[1,4096]{1,0:T(1,128)} %dist_hbm.1), custom_call_target="tpu_custom_call" | custom-call | flops 6000000000 | bytes 2000000 | tf_op jit(solution)/shard_map/pallas_call | solution.py:485
  26.8 0.6 %copy.9 = f32[16,1024]{1,0:T(8,128)} copy(f32[16,1024]{1,0:T(8,128)S(1)} %shard_map.73) | data formatting | bytes 131072

commit v4 on v3

--- a/solution.py
+++ b/solution.py
@@ -28,12 +28,15 @@
 HALF = COLS // 2
 TOEP_LO = -(BLOCKS - 1) * SUB - 128
 TOEP_WIDTH = (2 * BLOCKS - 1) * SUB + 128
+NEAR = 2
+NEAR_LO = -NEAR * SUB - 128
+NEAR_WIDTH = (2 * NEAR + 1) * SUB + 128
 TILE = 512
-FAR_FIRST = sorted(
-    ((dy, dz, dc) for dy in range(4) for dz in range(4) for dc in range(2)),
-    key=lambda at: (-min(at[0], 4 - at[0]) - min(at[1], 4 - at[1]), -at[2], at[0], at[1]),
+FAR_CHIPS = sorted(
+    ((dy, dz) for dy in range(4) for dz in range(4) if dy + dz > 0),
+    key=lambda at: (-min(at[0], 4 - at[0]) - min(at[1], 4 - at[1]), at),
 )
-TILE_ORDER = ((2, 1), (2, 0), (1, 1), (3, 1), (1, 0), (3, 0), (0, 1), (0, 0))
+FAR_LANE = [(2, 1), (2, 0), (1, 1), (1, 0), (3, 1), (3, 0), (0, 1), (0, 0)]
 
 
 def split_hi_lo(value):
@@ -47,29 +50,37 @@
     return (-1.0 / math.pi**2) / (step * step)
 
 
-def make_toeplitz(toep):
+def make_toeplitz(toep, toep_near):
     lane = lax.broadcasted_iota(I32, (128, 128), 1)
     sub = lax.broadcasted_iota(I32, (128, 128), 0)
     base = (2 * (lane - sub + TOEP_LO) - 1).astype(F32)
+    skip = (NEAR_LO - TOEP_LO) // 128
+
+    def value(tile):
+        step = base + 256.0 * tile.astype(F32)
+        square = step * step
+        guess = pltpu.reciprocal(square, approx=True)
+        return guess * (2.0 - square * guess) * (-1.0 / math.pi**2)
 
     def one(j, carry):
         for i in range(3):
             tile = j * 3 + i
-            step = base + 256.0 * tile.astype(F32)
-            square = step * step
-            guess = pltpu.reciprocal(square, approx=True)
-            guess = guess * (2.0 - square * guess)
-            high, low = split_hi_lo(guess * (-1.0 / math.pi**2))
-            where = pl.ds(pl.multiple_of(tile * 128, 128), 128)
-            toep[0, :, where] = high
-            toep[1, :, where] = low
+            toep[:, pl.ds(pl.multiple_of(tile * 128, 128), 128)] = value(tile).astype(BF16)
         return carry
 
+    def near(j, carry):
+        where = pl.ds(pl.multiple_of(j * 128, 128), 128)
+        high, low = split_hi_lo(value(j + skip))
+        toep_near[0, :, where] = high
+        toep_near[1, :, where] = low
+        return carry
+
     lax.fori_loop(0, TOEP_WIDTH // 384, one, 0)
+    lax.fori_loop(0, NEAR_WIDTH // 128, near, 0)
 
 
 def make_hot(n, col_d, hot_even, hot_odd):
-    lanes = pl.ds(pl.multiple_of(n * SUB, SUB), SUB)
+    lanes = slice(n * SUB, (n + 1) * SUB)
     column = col_d[:, lanes]
     row = lax.broadcasted_iota(I32, (SUB, SUB), 0).astype(F32).astype(BF16)
     one = jnp.ones((SUB, SUB), BF16)
@@ -139,25 +150,34 @@
         y_ref[mb * 32 + 16 : mb * 32 + 32, lanes] = quarter[src, 128:] + edge
 
 
-def convolve(col_d, toep, hot_even, hot_odd, z_ref, y_ref):
-    def one_pass(turn, carry):
-        z_at = turn % 2
-        t_at = turn // 2
-        for n in range(2 * BLOCKS - 1):
-            d = n - (BLOCKS - 1)
-            at = n * SUB + 128
-            count = (BLOCKS - abs(d)) * 32
-            src = slice(max(0, -d) * 32, max(0, -d) * 32 + count)
-            dst = slice(max(0, d) * 32, max(0, d) * 32 + count)
-            table = jnp.concatenate(
-                [toep[t_at, :, at : at + SUB], toep[t_at, :, at - 128 : at + 128]], axis=0
-            )
-            y_ref[dst, :] += jnp.dot(z_ref[z_at, src, :], table, preferred_element_type=F32)
-            if n % 5 == 2:
-                make_hot(jnp.minimum(turn * 6 + n // 5, VOX // SUB - 1), col_d, hot_even, hot_odd)
-        return carry
-
-    lax.fori_loop(0, 3, one_pass, 0)
+def add_block(d, count, table, z_part, y_ref):
+    src = max(0, -d) * 32
+    dst = max(0, d) * 32
+    y_ref[dst : dst + count, :] += jnp.dot(
+        z_part[src : src + count, :], table, preferred_element_type=F32
+    )
+
+
+def two_rows(toep, at):
+    return jnp.concatenate([toep[:, at : at + SUB], toep[:, at - 128 : at + 128]], axis=0)
+
+
+def convolve_far(col_d, toep, hot_even, hot_odd, z_ref, y_ref):
+    step = 0
+    for d in range(-(BLOCKS - 1), BLOCKS):
+        if abs(d) > NEAR:
+            table = two_rows(toep, d * SUB - TOEP_LO)
+            add_block(d, (BLOCKS - abs(d)) * 32, table, z_ref.at[0], y_ref)
+            if step < VOX // SUB:
+                make_hot(step, col_d, hot_even, hot_odd)
+            step += 1
+
+
+def convolve_near(toep_near, z_ref, y_ref):
+    for d in range(-NEAR, NEAR + 1):
+        for z_at, t_at in ((0, 0), (1, 0), (0, 1)):
+            table = two_rows(toep_near.at[t_at], d * SUB - NEAR_LO)
+            add_block(d, (BLOCKS - abs(d)) * 32, table, z_ref.at[z_at], y_ref)
 
 
 def round_filtered(y_ref, f_even, f_odd):
@@ -245,16 +265,14 @@
     return (1.0 - frac) * values[0] + frac * values[1]
 
 
-def look_up_half(th, st_ref, tables, o_send):
+def look_up_half(half, st_ref, tables, o_send):
     found = []
     for zh in range(2):
-        at = (zh * 2 + th) * 128
-        found.append(
-            [look_up(st_ref[v * 8 : v * 8 + 8, at : at + 128], tables, v) for v in range(16)]
-        )
+        lanes = pl.ds(pl.multiple_of((zh * 2 + half) * 128, 128), 128)
+        found.append([look_up(st_ref[v * 8 : v * 8 + 8, lanes], tables, v) for v in range(16)])
     for e in range(2):
         stack = jnp.concatenate(found[0][e * 8 : e * 8 + 8] + found[1][e * 8 : e * 8 + 8], axis=0)
-        o_send[e, th * 16 : th * 16 + 16] = stack.T.reshape(16, 8, 128)
+        o_send[e, pl.ds(half * 16, 16)] = stack.T.reshape(16, 8, 128)
 
 
 def sum_angles(o_recv, out_ref):
@@ -274,7 +292,7 @@
     x_hbm, start_hbm, rows_hbm, frac_hbm, col_hbm, colf_hbm, dist_hbm, out_ref,
     x_v, start_v, rows_v, frac_v, col_v, colf_v, dist_v,
     col_d, colf_d, dist_d,
-    toep, hot_even, hot_odd, xs_hi, xs_lo, z_ref, y_ref, f_even, f_odd,
+    toep, toep_near, hot_even, hot_odd, xs_hi, xs_lo, z_ref, y_ref, f_even, f_odd,
     s_send, s_recv, h_send, h_recv, o_send, o_recv, st_ref,
     in_sem, s_ssem, s_rsem, h_ssem, h_rsem, o_ssem, o_rsem, plane_sem,
 ):
@@ -287,10 +305,6 @@
     ys = [lax.rem(slab // 8 + dy, 4) * 8 for dy in range(4)]
     zs = [lax.rem(chip + dz, 4) * 2 for dz in range(4)]
     cores = (core, 1 - core)
-
-    def far_first(o):
-        dy, dz, dc = FAR_FIRST[o]
-        return ys[dy] + zs[dz] + cores[dc]
 
     loads = [
         pltpu.make_async_copy(src, dst, in_sem.at[i])
@@ -311,20 +325,23 @@
 
     barrier = pltpu.get_barrier_semaphore()
 
-    def greet(o, carry):
-        pl.semaphore_signal(
-            barrier, inc=1, device_id=(angle, far_first(o)), device_id_type=MESH
-        )
+    def greet(peer):
+        pl.semaphore_signal(barrier, inc=1, device_id=(angle, peer), device_id_type=MESH)
+
+    def greet_cores(turn, carry):
+        same = turn * core + (1 - turn) * (1 - core)
+        for dy, dz in FAR_CHIPS:
+            greet(ys[dy] + zs[dz] + same)
         return carry
 
-    for o in range(SLABS - 1):
-        greet(o, 0)
+    lax.fori_loop(0, 2, greet_cores, 0)
+    greet(slab + 1 - 2 * core)
     for o in range(1, ANGLES):
         pl.semaphore_signal(
             barrier, inc=1, device_id=(lax.rem(angle + o, ANGLES), slab), device_id_type=MESH
         )
 
-    make_toeplitz(toep)
+    make_toeplitz(toep, toep_near)
     for load in loads:
         load.wait()
     for src, dst in ((col_v, col_d), (colf_v, colf_d), (dist_v, dist_d)):
@@ -345,30 +362,42 @@
             device_id=(to_angle, to_slab), device_id_type=MESH,
         ).start()
 
-    def send_rows(o, carry):
-        peer = far_first(o)
+    def send_rows_to(peer):
         send(s_send.at[peer], s_recv.at[slab], s_ssem, s_rsem, angle, peer)
+
+    for dy, dz in FAR_CHIPS:
+        for dc in range(2):
+            send_rows_to(ys[dy] + zs[dz] + cores[dc])
+    send_rows_to(slab + 1 - 2 * core)
+    s_recv[slab] = s_send[slab]
+    convolve_far(col_d, toep, hot_even, hot_odd, z_ref, y_ref)
+    convolve_near(toep_near, z_ref, y_ref)
+    round_filtered(y_ref, f_even, f_odd)
+
+    def send_columns(peer):
+        send(h_send.at[peer], h_recv.at[slab], h_ssem, h_rsem, angle, peer)
+
+    def tile_at(dy, dz):
+        return lax.rem(slab // 8 + dy, 4) * 2 + lax.rem(slab // 4 + dz, 2)
+
+    def columns(turn, carry):
+        for i, (dy, dz) in enumerate(
+            ((2 + turn, 1), (2 + turn, 0), (1 - turn, 1), (1 - turn, 0))
+        ):
+            tile = tile_at(dy, dz)
+            at = pl.multiple_of(tile * TILE, TILE)
+            value = interpolate_columns(
+                at, f_even, f_odd, hot_even, hot_odd, col_d, colf_d, dist_d
+            ).astype(BF16)
+            for j in range(4):
+                h_send[tile * 4 + j] = value[:, j * 128 : (j + 1) * 128]
+            for j in range(4):
+                if i < 3 or j > 0:
+                    send_columns(tile * 4 + lax.rem(slab + j, 4))
         return carry
 
-    for o in range(SLABS - 1):
-        send_rows(o, 0)
-    s_recv[slab] = s_send[slab]
-
-    convolve(col_d, toep, hot_even, hot_odd, z_ref, y_ref)
-    round_filtered(y_ref, f_even, f_odd)
-
-    for i, (dy, dz) in enumerate(TILE_ORDER):
-        tile = lax.rem(slab // 8 + dy, 4) * 2 + lax.rem(slab // 4 + dz, 2)
-        at = pl.multiple_of(tile * TILE, TILE)
-        value = interpolate_columns(
-            at, f_even, f_odd, hot_even, hot_odd, col_d, colf_d, dist_d
-        ).astype(BF16)
-        for j in range(4):
-            h_send[tile * 4 + j] = value[:, j * 128 : (j + 1) * 128]
-        for j in range(4):
-            peer = tile * 4 + lax.rem(slab + j, 4)
-            if i < len(TILE_ORDER) - 1 or j > 0:
-                send(h_send.at[peer], h_recv.at[slab], h_ssem, h_rsem, angle, peer)
+    lax.fori_loop(0, 2, columns, 0)
+    send_columns(tile_at(1, 0) * 4 + lax.rem(slab, 4))
     h_recv[slab] = h_send[slab]
 
     def wait_bytes(ref, count, sem):
@@ -379,19 +408,21 @@
     pl.semaphore_wait(plane_sem, ANGLES - 1)
     wait_bytes(h_recv, SLABS - 1, h_rsem)
     tables = make_tables(h_recv)
-    for th in range(2):
-        look_up_half(th, st_ref, tables, o_send)
-
     slot = angle * 16 + chip
-
-    def send_planes(o, carry):
-        t = far_first(o)
-        for e in range(2):
-            send(o_send.at[e, t], o_recv.at[slot], o_ssem, o_rsem, core + 2 * e, t)
-        return carry
-
-    for o in range(SLABS - 1):
-        send_planes(o, 0)
+    my_half = slab // 16
+    own_y = slab // 8
+    other_y = my_half * 4 + 1 - own_y
+    for turn in range(2):
+        half = 1 - my_half if turn == 0 else my_half
+        look_up_half(half, st_ref, tables, o_send)
+        rows = (lax.rem(own_y + 2, 4), lax.rem(other_y + 2, 4)) if turn == 0 else (other_y, own_y)
+        for i in range(16):
+            dz, dc = FAR_LANE[i % 8]
+            if turn == 1 and i == 15:
+                break
+            t = rows[i // 8] * 8 + zs[dz] + cores[dc]
+            for e in range(2):
+                send(o_send.at[e, t], o_recv.at[slot], o_ssem, o_rsem, core + 2 * e, t)
     for e in range(2):
 
         @pl.when(core + 2 * e != angle)
@@ -432,7 +463,8 @@
     pltpu.VMEM((1, VOX), I32),
     pltpu.VMEM((1, VOX), F32),
     pltpu.VMEM((1, VOX), F32),
-    pltpu.VMEM((2, 128, TOEP_WIDTH), BF16),
+    pltpu.VMEM((128, TOEP_WIDTH), BF16),
+    pltpu.VMEM((2, 128, NEAR_WIDTH), BF16),
     pltpu.VMEM((SUB, VOX), BF16),
     pltpu.VMEM((SUB, VOX), BF16),
     pltpu.VMEM((2 * SUB + ROWS, SUB), BF16),

time: 27.5 us -> 26 us (0.945)
  Pallas kernels: 26.7 us -> 25.3 us
    pallas_call x1, Pallas kernels: 26.7 us -> 25.3 us  [body(): call(*(pltpu.with_memory_space_constraint(value, pltpu.HBM) for value in...]
where the time goes in v4:
time: 26 us; the launch traced here: 25.9 us
  Pallas kernels  25.3 us (97%)
  local copies, waits for them, and re-layouts  0.63 us (2%)
    pallas_call x1, Pallas kernels, body(): call(*(pltpu.with_memory_space_constraint(value, pltpu.HBM) for value in...  25.3 us
    unnamed x1, local copies, waits for them, and re-layouts  0.63 us

profile of v4, /device:TPU:1, one launch (start us, length us, event | category | flops | bytes accessed | tf_op | source)
XLA Modules:
  0.0 25.9 jit_solution(10610281233468152525)
XLA Ops:
  0.0 25.3 %shard_map.73 = f32[16,1024]{1,0:T(8,128)S(1)} custom-call(f32[4,4,8192]{2,1,0:T(4,128)} %bitcast.3, s32[1,32]{1,0:T(1,128)} %start_hbm.1, s32[16,4096]{1,0:T(8,128)} %bitcast.4, f32[16,4096]{1,0:T(8,128)} %bitcast.5, s32[1,4096]{1,0:T(1,128)} %col_hbm.1, f32[1,4096]{1,0:T(1,128)} %colf_hbm.1, f32[1,4096]{1,0:T(1,128)} %dist_hbm.1), custom_call_target="tpu_custom_call" | custom-call | flops 6000000000 | bytes 2000000 | tf_op jit(solution)/shard_map/pallas_call | solution.py:517
  25.3 0.6 %copy.9 = f32[16,1024]{1,0:T(8,128)} copy(f32[16,1024]{1,0:T(8,128)S(1)} %shard_map.73) | data formatting | bytes 131072

commit v5 on v4

--- a/solution.py
+++ b/solution.py
@@ -28,7 +28,7 @@
 HALF = COLS // 2
 TOEP_LO = -(BLOCKS - 1) * SUB - 128
 TOEP_WIDTH = (2 * BLOCKS - 1) * SUB + 128
-NEAR = 2
+NEAR = 1
 NEAR_LO = -NEAR * SUB - 128
 NEAR_WIDTH = (2 * NEAR + 1) * SUB + 128
 TILE = 512
@@ -57,26 +57,26 @@
     skip = (NEAR_LO - TOEP_LO) // 128
 
     def value(tile):
-        step = base + 256.0 * tile.astype(F32)
+        step = base + 256.0 * jnp.asarray(tile, I32).astype(F32)
         square = step * step
         guess = pltpu.reciprocal(square, approx=True)
         return guess * (2.0 - square * guess) * (-1.0 / math.pi**2)
 
     def one(j, carry):
-        for i in range(3):
-            tile = j * 3 + i
+        for i in range(9):
+            tile = j * 9 + i
             toep[:, pl.ds(pl.multiple_of(tile * 128, 128), 128)] = value(tile).astype(BF16)
         return carry
 
-    def near(j, carry):
-        where = pl.ds(pl.multiple_of(j * 128, 128), 128)
+    def near(j):
+        where = slice(j * 128, (j + 1) * 128)
         high, low = split_hi_lo(value(j + skip))
         toep_near[0, :, where] = high
         toep_near[1, :, where] = low
-        return carry
-
-    lax.fori_loop(0, TOEP_WIDTH // 384, one, 0)
-    lax.fori_loop(0, NEAR_WIDTH // 128, near, 0)
+
+    lax.fori_loop(0, TOEP_WIDTH // 1152, one, 0)
+    for j in range(NEAR_WIDTH // 128):
+        near(j)
 
 
 def make_hot(n, col_d, hot_even, hot_odd):
@@ -232,29 +232,34 @@
             s_send[2 * k + q % 2, :, half] = position[:, k * 64 : k * 64 + 64]
 
 
-def transpose_rows(s_recv, st_ref):
-    for zh in range(2):
-        for th in range(2):
-            block = s_recv[th * 16 : th * 16 + 16, zh * 8 : zh * 8 + 8, :].reshape(128, 128)
-            at = (zh * 2 + th) * 128
-            st_ref[:, at : at + 128] = block.T
+def transpose_rows(s_recv, st_ref, low_ref, high_ref):
+    def one(i, carry):
+        zh, th = i // 2, i % 2
+        block = s_recv[pl.ds(th * 16, 16), pl.ds(pl.multiple_of(zh * 8, 8), 8), :]
+        position = block.reshape(128, 128).T
+        row = position.astype(I32)
+        lanes = pl.ds(pl.multiple_of(i * 128, 128), 128)
+        st_ref[:, lanes] = position - row.astype(F32)
+        for ref, r in ((low_ref, row), (high_ref, jnp.minimum(row + 1, DET - 1))):
+            ref[:, lanes] = (
+                jnp.bitwise_and(lax.shift_right_logical(r, 2), 31) * 16
+                + lax.shift_right_logical(r, 7) * 4
+                + jnp.bitwise_and(r, 3)
+            )
+        return carry
+
+    lax.fori_loop(0, 4, one, 0)
 
 
 def make_tables(h_recv):
     return [h_recv[g * 8 : (g + 1) * 8].reshape(128, 128).astype(F32).T for g in range(4)]
 
 
-def look_up(position, tables, v):
-    row = position.astype(I32)
-    frac = position - row.astype(F32)
+def look_up(frac, places, tables, v):
     values = []
-    for r in (row, jnp.minimum(row + 1, DET - 1)):
-        lane = (
-            jnp.bitwise_and(lax.shift_right_logical(r, 2), 7) * 16
-            + lax.shift_right_logical(r, 7) * 4
-            + jnp.bitwise_and(r, 3)
-        )
-        which = jnp.bitwise_and(lax.shift_right_logical(r, 5), 3)
+    for place in places:
+        lane = jnp.bitwise_and(place, 127)
+        which = lax.shift_right_logical(place, 7)
         got = None
         for k in range(4):
             part = jnp.take_along_axis(
@@ -265,11 +270,16 @@
     return (1.0 - frac) * values[0] + frac * values[1]
 
 
-def look_up_half(half, st_ref, tables, o_send):
+def look_up_half(half, st_ref, low_ref, high_ref, tables, o_send):
     found = []
     for zh in range(2):
         lanes = pl.ds(pl.multiple_of((zh * 2 + half) * 128, 128), 128)
-        found.append([look_up(st_ref[v * 8 : v * 8 + 8, lanes], tables, v) for v in range(16)])
+        column = []
+        for v in range(16):
+            rows = slice(v * 8, v * 8 + 8)
+            places = (low_ref[rows, lanes], high_ref[rows, lanes])
+            column.append(look_up(st_ref[rows, lanes], places, tables, v))
+        found.append(column)
     for e in range(2):
         stack = jnp.concatenate(found[0][e * 8 : e * 8 + 8] + found[1][e * 8 : e * 8 + 8], axis=0)
         o_send[e, pl.ds(half * 16, 16)] = stack.T.reshape(16, 8, 128)
@@ -293,7 +303,7 @@
     x_v, start_v, rows_v, frac_v, col_v, colf_v, dist_v,
     col_d, colf_d, dist_d,
     toep, toep_near, hot_even, hot_odd, xs_hi, xs_lo, z_ref, y_ref, f_even, f_odd,
-    s_send, s_recv, h_send, h_recv, o_send, o_recv, st_ref,
+    s_send, s_recv, h_send, h_recv, o_send, o_recv, st_ref, low_ref, high_ref,
     in_sem, s_ssem, s_rsem, h_ssem, h_rsem, o_ssem, o_rsem, plane_sem,
 ):
     angle = lax.axis_index("angle")
@@ -320,9 +330,6 @@
             )
         )
     ]
-    for load in loads:
-        load.start()
-
     barrier = pltpu.get_barrier_semaphore()
 
     def greet(peer):
@@ -340,6 +347,9 @@
         pl.semaphore_signal(
             barrier, inc=1, device_id=(lax.rem(angle + o, ANGLES), slab), device_id_type=MESH
         )
+
+    for load in loads:
+        load.start()
 
     make_toeplitz(toep, toep_near)
     for load in loads:
@@ -365,12 +375,18 @@
     def send_rows_to(peer):
         send(s_send.at[peer], s_recv.at[slab], s_ssem, s_rsem, angle, peer)
 
-    for dy, dz in FAR_CHIPS:
-        for dc in range(2):
-            send_rows_to(ys[dy] + zs[dz] + cores[dc])
-    send_rows_to(slab + 1 - 2 * core)
-    s_recv[slab] = s_send[slab]
-    convolve_far(col_d, toep, hot_even, hot_odd, z_ref, y_ref)
+    @pl.when(slab < SLABS)
+    def _():
+        for dy, dz in FAR_CHIPS:
+            for dc in range(2):
+                send_rows_to(ys[dy] + zs[dz] + cores[dc])
+        send_rows_to(slab + 1 - 2 * core)
+        s_recv[slab] = s_send[slab]
+
+    @pl.when(slab < SLABS)
+    def _():
+        convolve_far(col_d, toep, hot_even, hot_odd, z_ref, y_ref)
+
     convolve_near(toep_near, z_ref, y_ref)
     round_filtered(y_ref, f_even, f_odd)
 
@@ -404,7 +420,7 @@
         pltpu.make_async_copy(ref.at[pl.ds(0, count)], ref.at[pl.ds(0, count)], sem).wait()
 
     wait_bytes(s_recv, SLABS - 1, s_rsem)
-    transpose_rows(s_recv, st_ref)
+    transpose_rows(s_recv, st_ref, low_ref, high_ref)
     pl.semaphore_wait(plane_sem, ANGLES - 1)
     wait_bytes(h_recv, SLABS - 1, h_rsem)
     tables = make_tables(h_recv)
@@ -414,7 +430,7 @@
     other_y = my_half * 4 + 1 - own_y
     for turn in range(2):
         half = 1 - my_half if turn == 0 else my_half
-        look_up_half(half, st_ref, tables, o_send)
+        look_up_half(half, st_ref, low_ref, high_ref, tables, o_send)
         rows = (lax.rem(own_y + 2, 4), lax.rem(other_y + 2, 4)) if turn == 0 else (other_y, own_y)
         for i in range(16):
             dz, dc = FAR_LANE[i % 8]
@@ -480,6 +496,8 @@
     pltpu.VMEM((2, SLABS, 8, 128), F32),
     pltpu.VMEM((2 * SLABS, 8, 128), F32),
     pltpu.VMEM((128, SLABS * PLANES), F32),
+    pltpu.VMEM((128, SLABS * PLANES), I32),
+    pltpu.VMEM((128, SLABS * PLANES), I32),
     pltpu.SemaphoreType.DMA((7,)),
     pltpu.SemaphoreType.DMA,
     pltpu.SemaphoreType.DMA,

time: 26 us -> 25.3 us (0.973)
  Pallas kernels: 25.3 us -> 24.5 us
    pallas_call x1, Pallas kernels: 25.3 us -> 24.5 us  [body(): call(*(pltpu.with_memory_space_constraint(value, pltpu.HBM) for value in...]
where the time goes in v5:
time: 25.3 us; the launch traced here: 25.2 us
  Pallas kernels  24.5 us (97%)
  local copies, waits for them, and re-layouts  0.63 us (2%)
    pallas_call x1, Pallas kernels, body(): call(*(pltpu.with_memory_space_constraint(value, pltpu.HBM) for value in...  24.5 us
    unnamed x1, local copies, waits for them, and re-layouts  0.63 us

profile of v5, /device:TPU:1, one launch (start us, length us, event | category | flops | bytes accessed | tf_op | source)
XLA Modules:
  0.0 25.2 jit_solution(13677445471241693289)
XLA Ops:
  0.0 24.5 %shard_map.73 = f32[16,1024]{1,0:T(8,128)S(1)} custom-call(f32[4,4,8192]{2,1,0:T(4,128)} %bitcast.3, s32[1,32]{1,0:T(1,128)} %start_hbm.1, s32[16,4096]{1,0:T(8,128)} %bitcast.4, f32[16,4096]{1,0:T(8,128)} %bitcast.5, s32[1,4096]{1,0:T(1,128)} %col_hbm.1, f32[1,4096]{1,0:T(1,128)} %colf_hbm.1, f32[1,4096]{1,0:T(1,128)} %dist_hbm.1), custom_call_target="tpu_custom_call" | custom-call | flops 6000000000 | bytes 2000000 | tf_op jit(solution)/shard_map/pallas_call | solution.py:535
  24.5 0.6 %copy.9 = f32[16,1024]{1,0:T(8,128)} copy(f32[16,1024]{1,0:T(8,128)S(1)} %shard_map.73) | data formatting | bytes 131072

commit v6 on v5

--- a/solution.py
+++ b/solution.py
@@ -168,16 +168,20 @@
         if abs(d) > NEAR:
             table = two_rows(toep, d * SUB - TOEP_LO)
             add_block(d, (BLOCKS - abs(d)) * 32, table, z_ref.at[0], y_ref)
-            if step < VOX // SUB:
+            if BLOCKS - abs(d) > 10:
                 make_hot(step, col_d, hot_even, hot_odd)
-            step += 1
-
-
-def convolve_near(toep_near, z_ref, y_ref):
+                step += 1
+
+
+def convolve_near(col_d, toep_near, hot_even, hot_odd, z_ref, y_ref):
+    step = VOX // SUB // 2
     for d in range(-NEAR, NEAR + 1):
         for z_at, t_at in ((0, 0), (1, 0), (0, 1)):
             table = two_rows(toep_near.at[t_at], d * SUB - NEAR_LO)
             add_block(d, (BLOCKS - abs(d)) * 32, table, z_ref.at[z_at], y_ref)
+            if step < VOX // SUB:
+                make_hot(step, col_d, hot_even, hot_odd)
+            step += 1
 
 
 def round_filtered(y_ref, f_even, f_odd):
@@ -387,7 +391,7 @@
     def _():
         convolve_far(col_d, toep, hot_even, hot_odd, z_ref, y_ref)
 
-    convolve_near(toep_near, z_ref, y_ref)
+    convolve_near(col_d, toep_near, hot_even, hot_odd, z_ref, y_ref)
     round_filtered(y_ref, f_even, f_odd)
 
     def send_columns(peer):

time: 25.3 us -> 25.2 us (level)
  no operation moved by 1% of the time
where the time goes in v6:
time: 25.2 us; the launch traced here: 25.1 us
  Pallas kernels  24.4 us (97%)
  local copies, waits for them, and re-layouts  0.63 us (2%)
    pallas_call x1, Pallas kernels, body(): call(*(pltpu.with_memory_space_constraint(value, pltpu.HBM) for value in...  24.4 us
    unnamed x1, local copies, waits for them, and re-layouts  0.63 us

profile of v6, /device:TPU:1, one launch (start us, length us, event | category | flops | bytes accessed | tf_op | source)
XLA Modules:
  0.0 25.1 jit_solution(7244747651617397848)
XLA Ops:
  0.0 24.4 %shard_map.73 = f32[16,1024]{1,0:T(8,128)S(1)} custom-call(f32[4,4,8192]{2,1,0:T(4,128)} %bitcast.3, s32[1,32]{1,0:T(1,128)} %start_hbm.1, s32[16,4096]{1,0:T(8,128)} %bitcast.4, f32[16,4096]{1,0:T(8,128)} %bitcast.5, s32[1,4096]{1,0:T(1,128)} %col_hbm.1, f32[1,4096]{1,0:T(1,128)} %colf_hbm.1, f32[1,4096]{1,0:T(1,128)} %dist_hbm.1), custom_call_target="tpu_custom_call" | custom-call | flops 6000000000 | bytes 2000000 | tf_op jit(solution)/shard_map/pallas_call | solution.py:539
  24.5 0.6 %copy.9 = f32[16,1024]{1,0:T(8,128)} copy(f32[16,1024]{1,0:T(8,128)S(1)} %shard_map.73) | data formatting | bytes 131072

commit v7 on v5

--- a/solution.py
+++ b/solution.py
@@ -120,16 +120,15 @@
     k = lax.broadcasted_iota(I32, (SUB, SUB), 0)
     n = lax.broadcasted_iota(I32, (SUB, SUB), 1)
     even_odd = one_hot(k == jnp.where(n < 128, 2 * n, 2 * n - 255))
-    k2 = lax.broadcasted_iota(I32, (2 * SUB, 128), 0)
-    n2 = lax.broadcasted_iota(I32, (2 * SUB, 128), 1)
-    later = one_hot(k2 == 2 * n2 + 2)
+    last_lane = lax.broadcasted_iota(I32, (2 * SUB, 128), 1) == 127
     first = None
     quarter = None
     for part, xs in enumerate((xs_hi, xs_lo)):
         here = xs[: 2 * SUB, :]
-        both = jnp.concatenate([here, xs[ROWS : 2 * SUB + ROWS, :]], axis=1)
         eo = jnp.dot(here, even_odd, preferred_element_type=F32)
-        es = jnp.dot(both, later, preferred_element_type=F32).astype(BF16)
+        turned = pltpu.roll(eo[:, :128], 127, 1)
+        following = jnp.concatenate([turned[ROWS:], jnp.zeros((ROWS, 128), F32)], axis=0)
+        es = jnp.where(last_lane, following, turned).astype(BF16)
         eo_b = eo[:, 128:].astype(BF16)
         for kb in range(2 * BLOCKS):
             mb, half = kb // 2, kb % 2

time: 25.3 us -> 25.3 us (level)
  no operation moved by 1% of the time
where the time goes in v7:
time: 25.3 us; the launch traced here: 25.2 us
  Pallas kernels  24.5 us (97%)
  local copies, waits for them, and re-layouts  0.63 us (2%)
    pallas_call x1, Pallas kernels, body(): call(*(pltpu.with_memory_space_constraint(value, pltpu.HBM) for value in...  24.5 us
    unnamed x1, local copies, waits for them, and re-layouts  0.63 us

profile of v7, /device:TPU:1, one launch (start us, length us, event | category | flops | bytes accessed | tf_op | source)
XLA Modules:
  0.0 25.2 jit_solution(17801256990246672376)
XLA Ops:
  0.0 24.5 %shard_map.73 = f32[16,1024]{1,0:T(8,128)S(1)} custom-call(f32[4,4,8192]{2,1,0:T(4,128)} %bitcast.3, s32[1,32]{1,0:T(1,128)} %start_hbm.1, s32[16,4096]{1,0:T(8,128)} %bitcast.4, f32[16,4096]{1,0:T(8,128)} %bitcast.5, s32[1,4096]{1,0:T(1,128)} %col_hbm.1, f32[1,4096]{1,0:T(1,128)} %colf_hbm.1, f32[1,4096]{1,0:T(1,128)} %dist_hbm.1), custom_call_target="tpu_custom_call" | custom-call | flops 6000000000 | bytes 2000000 | tf_op jit(solution)/shard_map/pallas_call | solution.py:534
  24.5 0.6 %copy.9 = f32[16,1024]{1,0:T(8,128)} copy(f32[16,1024]{1,0:T(8,128)S(1)} %shard_map.73) | data formatting | bytes 131072
